TPU v7x, 128 devices: a whole 4x4x4 slice. The times are simulated.
128 devices in a mesh: gx: 8 (over y, core), gy: 16 (over z, x).
Axes of the slice: x: 4, y: 4, z: 4, core: 2. Of those that a mesh axis runs over, the one named last changes fastest.
Arguments:
- rhs_matrix: float32 [2048, 2048], P('gx', 'gy'), may hold values from -6 to 6
- trans_x: float32 [2048, 2048], P('gx', 'gy'), may hold values from 0.2 to 5
- trans_y: float32 [2048, 2048], P('gx', 'gy'), may hold values from 0.2 to 5
- leak_matrix: float32 [2048, 2048], P('gx', 'gy'), may hold values from 0.02 to 0.2
- rhs_fracture: float32 [16384, 128], P(('gx', 'gy')), may hold values from -6 to 6
- trans_frac: float32 [16384, 128], P(('gx', 'gy')), may hold values from 2 to 50
- store_frac: float32 [16384, 128], P(('gx', 'gy')), may hold values from 0.05 to 0.5
- mortar_coef: float32 [16384, 128], P(('gx', 'gy')), may hold values from 0.2 to 5
- block_home: int32 [16384, 1], P(('gx', 'gy')), may hold values from 0 to 127; in each aligned block of 128 rows (0 to 127, 128 to 255, ...) at most 2 rows name the same one
- block_len: int32 [16384], P(('gx', 'gy')), may hold values from 1 to 128, 1572864 in all
- mortar_cell: int32 [16384, 1], P(('gx', 'gy')), may hold values from 0 to 63
- cross_cell: int32 [16384, 2], P(('gx', 'gy')), may hold values from 0 to 127
- cross_partner: int32 [16384, 2], P(('gx', 'gy')), may hold values from 0 to 16383
- cross_trans: float32 [16384, 2], P(('gx', 'gy')), may hold values from 0.5 to 5
Outputs:
- pressure_matrix: float32 [2048, 2048], P('gx', 'gy')
- pressure_fracture: float32 [16384, 128], P(('gx', 'gy'))
- mortar_flux: float32 [16384, 128], P(('gx', 'gy'))
Inputs may be any that keep to these rules, and one draw needn't show every extreme that they name: `block_home`: among the 128 blocks stored on one device (aligned blocks of rows), no tile is named more than 2 times, a bound that some block reaches. Tile t holds grid rows 256 * (t // 16) onward and grid columns 128 * (t % 16) onward. Cells c >= block_len[b] of block b are padding. `mortar_cell`: segment m covers row m of the home tile, all of its 128 columns; the fractures cross the first 64 rows of a tile. `cross_partner`: index k * 128 + c of cell c of the k-th block of the group of 128 blocks b // 128 that holds block b.
All inputs are finite; a program needn't handle non-finite values.
Results may differ from a plain program's by a relative error of at most 0.00012.
Values sent between devices are 32-bit elements; how exact they have to be, the bound alone decides.
A program may use at most 64 MiB of HBM per device.

v0:
```python
import jax
import jax.numpy as jnp
from jax import lax
from jax.sharding import PartitionSpec as P

ITERS = 3


highest = lax.Precision.HIGHEST


def shifted(array, axis, by):
    count = lax.axis_size(axis)
    pairs = [(i, i + by) for i in range(count) if 0 <= i + by < count]
    return lax.ppermute(array, axis, pairs)


def extended(array, sides, width):
    for axis, dim in sides:
        count, length = (lax.axis_size(axis), array.shape[dim])
        up = [(i, (i + 1) % count) for i in range(count - 1)]
        down = [(j, i) for i, j in up]
        last = lax.slice_in_dim(array, length - width, length, axis=dim)
        initial = lax.slice_in_dim(array, 0, width, axis=dim)
        before = lax.ppermute(last, axis, up)
        after = lax.ppermute(initial, axis, down)
        array = jnp.concatenate([before, array, after], axis=dim)
    return array


def previous_cols(field):
    return jnp.concatenate([jnp.zeros_like(field[:, :1]), field[:, :-1]], 1)


def next_cols(field):
    return jnp.concatenate([field[:, 1:], jnp.zeros_like(field[:, :1])], 1)


def inner_local(former, latter):
    return (
        jnp.sum(former[0] * latter[0])
        + jnp.sum(former[1] * latter[1])
        + jnp.sum(former[2] * latter[2])
    )


def global_dot(former, latter):
    return lax.psum(inner_local(former, latter), ("gx", "gy"))


def three_term(image, lanczos_now, lanczos_old, coef_now, coef_old):
    return tuple(
        (
            part_image - coef_now * part_now - coef_old * part_old
            for part_image, part_now, part_old in zip(image, lanczos_now, lanczos_old)
        )
    )


def search_update(precond_now, search_old, search_now, alpha_three, alpha_two, alpha_one):
    return tuple(
        (
            (part_z - alpha_three * part_old - alpha_two * part_now) / alpha_one
            for part_z, part_old, part_now in zip(precond_now, search_old, search_now)
        )
    )


def local(
    rhs_matrix,
    trans_x,
    trans_y,
    leak_matrix,
    rhs_fracture,
    trans_frac,
    store_frac,
    mortar_coef,
    block_home,
    block_len,
    mortar_cell,
    cross_cell,
    cross_partner,
    cross_trans,
):
    num_blocks, block_width = rhs_fracture.shape
    tile_rows, tile_cols = rhs_matrix.shape
    num_cross = cross_cell.shape[1]
    devices = lax.axis_size(("gx", "gy"))
    capacity = 2 * num_blocks // devices
    num_slots = devices * capacity
    band_rows = tile_rows // 4
    num_segments = band_rows * (tile_cols // block_width)
    positions = lax.broadcasted_iota(jnp.int32, rhs_fracture.shape, 1)
    cell_mask = (positions < block_len[:, None]).astype(jnp.float32)
    face_trans = trans_frac * cell_mask * next_cols(cell_mask)
    face_prev = previous_cols(face_trans)
    storage = store_frac * cell_mask
    cell_iota = lax.broadcasted_iota(jnp.int32, (num_blocks, num_cross, block_width), 2)
    own_hot = (cell_iota == cross_cell[:, :, None]).astype(jnp.float32)
    partner_block = cross_partner // block_width
    partner_hot = (cell_iota == (cross_partner % block_width)[:, :, None]).astype(jnp.float32)
    block_iota = lax.broadcasted_iota(jnp.int32, (num_blocks * num_cross, num_blocks), 1)
    partner_rows = (block_iota == partner_block.reshape(-1)[:, None]).astype(jnp.float32)

    def pick_own(field):
        return jnp.sum(own_hot * field[:, None, :], axis=2)

    def pick_partner(field):
        return jnp.sum(field[partner_block] * partner_hot, axis=2)

    def spread_cross(own_values, partner_values):
        own_part = jnp.sum(own_hot * own_values[:, :, None], axis=1)
        pieces = (partner_hot * partner_values[:, :, None]).reshape(
            num_blocks * num_cross, block_width
        )
        partner_part = jnp.dot(
            partner_rows.T, pieces, precision=highest, preferred_element_type=jnp.float32
        )
        return own_part + partner_part

    cross_weight = cross_trans * pick_own(cell_mask) * pick_partner(cell_mask)
    home_tile = block_home[:, 0]
    row_index = lax.broadcasted_iota(jnp.int32, (num_blocks, num_blocks), 0)
    col_index = lax.broadcasted_iota(jnp.int32, (num_blocks, num_blocks), 1)
    earlier = (home_tile[None, :] == home_tile[:, None]) & (col_index < row_index)
    slot_rank = jnp.sum(earlier.astype(jnp.int32), axis=1)
    target = home_tile * capacity + slot_rank
    slot_iota = lax.broadcasted_iota(jnp.int32, (num_slots, num_blocks), 0)
    slot_match = slot_iota == target[None, :]
    slot_hot = slot_match.astype(jnp.float32)
    cell_lists = jnp.sum(
        jnp.where(slot_match, mortar_cell[:, 0][None, :], 0), axis=1, keepdims=True
    )
    requests = lax.all_to_all(cell_lists, ("gx", "gy"), split_axis=0, concat_axis=0, tiled=True)
    segment_iota = lax.broadcasted_iota(jnp.int32, (num_slots, num_segments), 1)
    request_hot = (segment_iota == requests).astype(jnp.float32)
    above_row = shifted(trans_x[-1:, :], "gx", 1)
    left_col = shifted(trans_y[:, -1:], "gy", 1)
    tx_prev = jnp.concatenate([above_row, trans_x[:-1]], 0)
    ty_prev = jnp.concatenate([left_col, trans_y[:, :-1]], 1)
    diag_matrix = leak_matrix + trans_x + tx_prev + trans_y + ty_prev
    diag_frac = storage + face_trans + face_prev + spread_cross(cross_weight, cross_weight)
    safe_frac = diag_frac + 1.0 - cell_mask
    inverse = (
        1.0 / diag_matrix,
        cell_mask / safe_frac,
        cell_mask / (1.0 / mortar_coef + 1.0 / safe_frac),
    )

    def precondition(vector):
        return tuple((part_inv * part_vec for part_inv, part_vec in zip(inverse, vector)))

    zero_vec = (
        jnp.zeros_like(rhs_matrix),
        jnp.zeros_like(rhs_fracture),
        jnp.zeros_like(rhs_fracture),
    )
    lanczos_now = (rhs_matrix, rhs_fracture * cell_mask, jnp.zeros_like(rhs_fracture))
    lanczos_old = zero_vec
    precond_now = precondition(lanczos_now)
    gamma_now = jnp.sqrt(global_dot(precond_now, lanczos_now))
    gamma_old = jnp.float32(1.0)
    rhs_scale = gamma_now
    cos_old = jnp.float32(1.0)
    cos_now = jnp.float32(1.0)
    sin_old = jnp.float32(0.0)
    sin_now = jnp.float32(0.0)
    search_old = zero_vec
    search_now = zero_vec
    iterate = zero_vec
    for step in range(ITERS):
        precond_now = tuple((part_z / gamma_now for part_z in precond_now))
        field_m, field_f, flux = precond_now
        padded = extended(field_m, (("gx", 0), ("gy", 1)), 1)
        outgoing = jnp.dot(slot_hot, flux, precision=highest, preferred_element_type=jnp.float32)
        segments = field_m[:band_rows]
        samples = jnp.dot(
            request_hot, segments, precision=highest, preferred_element_type=jnp.float32
        )
        arrived = lax.all_to_all(
            jnp.stack([outgoing, samples]), ("gx", "gy"), split_axis=1, concat_axis=1, tiled=True
        )
        out_m = (
            leak_matrix * field_m
            + trans_x * (field_m - padded[2:, 1:-1])
            + tx_prev * (field_m - padded[:-2, 1:-1])
            + trans_y * (field_m - padded[1:-1, 2:])
            + ty_prev * (field_m - padded[1:-1, :-2])
        )
        added = jnp.dot(
            request_hot.T, arrived[0], precision=highest, preferred_element_type=jnp.float32
        )
        out_m = jnp.concatenate([out_m[:band_rows] + added, out_m[band_rows:]], 0)
        sampled = jnp.dot(
            slot_hot.T, arrived[1], precision=highest, preferred_element_type=jnp.float32
        )
        jump_term = cross_weight * (pick_own(field_f) - pick_partner(field_f))
        out_f = (
            storage * field_f
            + face_trans * (field_f - next_cols(field_f))
            + face_prev * (field_f - previous_cols(field_f))
            + spread_cross(jump_term, -jump_term)
            - flux
        )
        out_l = cell_mask * (sampled - field_f - flux / mortar_coef)
        image = (out_m, out_f, out_l)
        curvature = global_dot(image, precond_now)
        lanczos_new = three_term(
            image, lanczos_now, lanczos_old, curvature / gamma_now, gamma_now / gamma_old
        )
        precond_new = precondition(lanczos_new)
        gamma_new = jnp.sqrt(global_dot(precond_new, lanczos_new))
        alpha_zero = cos_now * curvature - cos_old * sin_now * gamma_now
        alpha_one = jnp.sqrt(alpha_zero * alpha_zero + gamma_new * gamma_new)
        alpha_two = sin_now * curvature + cos_old * cos_now * gamma_now
        alpha_three = sin_old * gamma_now
        cos_new = alpha_zero / alpha_one
        sin_new = gamma_new / alpha_one
        search_new = search_update(
            precond_now, search_old, search_now, alpha_three, alpha_two, alpha_one
        )
        iterate = tuple(
            (part_x + cos_new * rhs_scale * part_w for part_x, part_w in zip(iterate, search_new))
        )
        rhs_scale = -sin_new * rhs_scale
        lanczos_old, lanczos_now = (lanczos_now, lanczos_new)
        precond_now = precond_new
        gamma_old, gamma_now = (gamma_now, gamma_new)
        cos_old, cos_now = (cos_now, cos_new)
        sin_old, sin_now = (sin_now, sin_new)
        search_old, search_now = (search_now, search_new)
    return (iterate[0], iterate[1], iterate[2])


def solution(mesh):
    return jax.shard_map(
        local,
        mesh=mesh,
        in_specs=(
            P("gx", "gy"),
            P("gx", "gy"),
            P("gx", "gy"),
            P("gx", "gy"),
            P(("gx", "gy"), None),
            P(("gx", "gy"), None),
            P(("gx", "gy"), None),
            P(("gx", "gy"), None),
            P(("gx", "gy"), None),
            P(("gx", "gy")),
            P(("gx", "gy"), None),
            P(("gx", "gy"), None),
            P(("gx", "gy"), None),
            P(("gx", "gy"), None),
        ),
        out_specs=(P("gx", "gy"), P(("gx", "gy"), None), P(("gx", "gy"), None)),
        check_vma=False,
    )
```

profile of v0, /device:TPU:1, one launch (start us, length us, event | category | flops | bytes accessed | tf_op | source)
XLA Modules:
  0.0 604.0 jit_solution(16565652828133881199)
XLA Ops:
  1.4 4.6 collective-permute-start
  9.1 9.8 %all-to-all-start = ((s32[128,2,1]{1,2,0:T(1,128)}), s32[128,2,1]{1,2,0:T(1,128)S(1)}, u32[]{:S(2)}, u32[]{:S(2)}) async-start(s32[128,2,1]{1,2,0:T(1,128)} %bitcast.3), calls=%async_computation | async-start | bytes 131072 | tf_op jit(solution)/shard_map/all_to_all | solution.py:134
  19.0 3.3 collective-permute-start.1
  28.7 1.0 multiply_reduce_fusion.17
  33.9 65.9 %psum.49 = f32[]{:T(128)} all-reduce(f32[]{:T(128)S(6)} %add.252), channel_id=1, replica_groups=mesh['gx'=8,'gy'=16] {'gx','gy'}, use_global_device_ids=true, to_apply=%region_6.7 | all-reduce | flops 1 | bytes 8 | tf_op jit(solution)/shard_map/psum | solution.py:48
  101.9 2.6 collective-permute-start.3
  104.5 1.9 collective-permute-start.2
  108.7 6.5 %all-to-all-start.1 = ((f32[2,256,128]{2,0,1:T(2,128)}), f32[2,256,128]{2,0,1:T(2,128)S(1)}, u32[]{:S(2)}, u32[]{:S(2)}) async-start(f32[2,256,128]{2,0,1:T(2,128)} %copy.53), calls=%async_computation.1 | async-start | bytes 524288 | tf_op jit(solution)/shard_map/all_to_all | solution.py:180
  115.3 1.3 collective-permute-start.4
  116.6 4.0 collective-permute-start.5
  120.6 1.0 multiply_reduce_fusion.15
  122.8 3.9 all-to-all-done.1
  130.7 68.1 %psum.50 = f32[]{:T(128)} all-reduce(f32[]{:T(128)S(6)} %add.264), channel_id=1, replica_groups=mesh['gx'=8,'gy'=16] {'gx','gy'}, use_global_device_ids=true, to_apply=%region_15.16 | all-reduce | flops 1 | bytes 8 | tf_op jit(solution)/shard_map/psum | solution.py:48
  203.5 63.3 %psum.51 = f32[]{:T(128)} all-reduce(f32[]{:T(128)S(6)} %add.266), channel_id=1, replica_groups=mesh['gx'=8,'gy'=16] {'gx','gy'}, use_global_device_ids=true, to_apply=%region_19.20 | all-reduce | flops 1 | bytes 8 | tf_op jit(solution)/shard_map/psum | solution.py:48
  269.1 2.5 collective-permute-start.7
  271.5 1.9 collective-permute-start.6
  274.6 5.7 all-to-all-start.2
  281.3 1.3 collective-permute-start.8
  282.6 4.0 collective-permute-start.9
  286.6 1.0 multiply_reduce_fusion.11
  289.3 2.4 all-to-all-done.2
  295.8 69.0 %psum.52 = f32[]{:T(128)} all-reduce(f32[]{:T(128)S(6)} %add.279), channel_id=1, replica_groups=mesh['gx'=8,'gy'=16] {'gx','gy'}, use_global_device_ids=true, to_apply=%region_26.27 | all-reduce | flops 1 | bytes 8 | tf_op jit(solution)/shard_map/psum | solution.py:48
  369.5 63.1 %psum.53 = f32[]{:T(128)} all-reduce(f32[]{:T(128)S(6)} %add.281), channel_id=1, replica_groups=mesh['gx'=8,'gy'=16] {'gx','gy'}, use_global_device_ids=true, to_apply=%region_30.31 | all-reduce | flops 1 | bytes 8 | tf_op jit(solution)/shard_map/psum | solution.py:48
  436.2 2.5 collective-permute-start.11
  438.6 1.9 collective-permute-start.10
  441.8 5.7 all-to-all-start.3
  447.7 1.3 collective-permute-start.12
  449.0 4.0 collective-permute-start.13
  453.0 1.0 multiply_reduce_fusion.7
  455.7 3.3 all-to-all-done.3
  463.1 68.9 %psum.54 = f32[]{:T(128)} all-reduce(f32[]{:T(128)S(6)} %add.295), channel_id=1, replica_groups=mesh['gx'=8,'gy'=16] {'gx','gy'}, use_global_device_ids=true, to_apply=%region_37.38 | all-reduce | flops 1 | bytes 8 | tf_op jit(solution)/shard_map/psum | solution.py:48
  538.0 63.1 %psum.55 = f32[]{:T(128)} all-reduce(f32[]{:T(128)S(6)} %add.297), channel_id=1, replica_groups=mesh['gx'=8,'gy'=16] {'gx','gy'}, use_global_device_ids=true, to_apply=%region_41.42 | all-reduce | flops 1 | bytes 8 | tf_op jit(solution)/shard_map/psum | solution.py:48
  (150 shorter events, 39.9 us)
Async XLA Ops:
  0.6 18.3 %copy-start.1 = (f32[256,128]{1,0:T(8,128)S(1)}, f32[256,128]{1,0:T(8,128)}, u32[]{:S(2)}) copy-start(f32[256,128]{1,0:T(8,128)} %param.16) | copy-start | bytes 393220
  1.4 29.7 %collective-permute-start = (f32[1,128]{1,0:T(1,128)S(1)}, f32[1,128]{1,0:T(1,128)S(1)}, u32[]{:S(2)}, u32[]{:S(2)}) collective-permute-start(f32[1,128]{1,0:T(1,128)S(1)} %slice.165), channel_id=1, source_target_pairs={{0,16},{16,32},{32,48},{48,64},{64,80},{80,96},{96,112},{1,17},{17... | collective-permute-start | bytes 1544 | tf_op jit(solution)/shard_map/ppermute | solution.py:15
  9.1 20.6 %all-to-all-start = ((s32[128,2,1]{1,2,0:T(1,128)}), s32[128,2,1]{1,2,0:T(1,128)S(1)}, u32[]{:S(2)}, u32[]{:S(2)}) async-start(s32[128,2,1]{1,2,0:T(1,128)} %bitcast.3), calls=%async_computation | async-start | bytes 131072 | tf_op jit(solution)/shard_map/all_to_all | solution.py:134
  18.9 3.4 copy-start.13
  19.0 12.0 %collective-permute-start.1 = (f32[256,1]{1,0:T(8,128)S(1)}, f32[256,1]{1,0:T(8,128)S(1)}, u32[]{:S(2)}, u32[]{:S(2)}) collective-permute-start(f32[256,1]{1,0:T(8,128)S(1)} %slice.167), channel_id=1, source_target_pairs={{0,1},{1,2},{2,3},{3,4},{4,5},{5,6},{6,7},{7,8},{8,9},{9,10},{10,1... | collective-permute-start | bytes 3080 | tf_op jit(solution)/shard_map/ppermute | solution.py:15
  22.6 0.7 copy-start.11
  23.5 0.7 copy-start.10
  24.3 0.7 copy-start.12
  26.9 0.8 copy-start.5
  27.8 0.8 copy-start.4
  27.8 0.9 copy-start.6
  27.8 0.9 copy-start.8
  28.7 2.4 copy-start.2
  28.7 2.4 copy-start.3
  29.7 1.4 copy-start
  101.9 13.3 %collective-permute-start.3 = (f32[1,128]{1,0:T(1,128)S(1)}, f32[1,128]{1,0:T(1,128)S(1)}, u32[]{:S(2)}, u32[]{:S(2)}) collective-permute-start(f32[1,128]{1,0:T(1,128)S(1)} %get-tuple-element.45), channel_id=1, source_target_pairs={{0,16},{16,32},{32,48},{48,64},{64,80},{80,96},{96,112},{1,17},{17... | collective-permute-start | bytes 1544 | tf_op jit(solution)/shard_map/ppermute | solution.py:25
  104.5 10.7 %collective-permute-start.2 = (f32[1,128]{1,0:T(1,128)S(1)}, f32[1,128]{1,0:T(1,128)S(1)}, u32[]{:S(2)}, u32[]{:S(2)}) collective-permute-start(f32[1,128]{1,0:T(1,128)S(1)} %get-tuple-element.46), channel_id=1, source_target_pairs={{16,0},{32,16},{48,32},{64,48},{80,64},{96,80},{112,96},{17,1},{33... | collective-permute-start | bytes 1544 | tf_op jit(solution)/shard_map/ppermute | solution.py:26
  108.7 17.9 %all-to-all-start.1 = ((f32[2,256,128]{2,0,1:T(2,128)}), f32[2,256,128]{2,0,1:T(2,128)S(1)}, u32[]{:S(2)}, u32[]{:S(2)}) async-start(f32[2,256,128]{2,0,1:T(2,128)} %copy.53), calls=%async_computation.1 | async-start | bytes 524288 | tf_op jit(solution)/shard_map/all_to_all | solution.py:180
  115.3 6.3 %collective-permute-start.4 = (f32[258,1]{1,0:T(8,128)S(1)}, f32[258,1]{1,0:T(8,128)S(1)}, u32[]{:S(2)}, u32[]{:S(2)}) collective-permute-start(f32[258,1]{1,0:T(8,128)S(1)} %get-tuple-element.39), channel_id=1, source_target_pairs={{1,0},{2,1},{3,2},{4,3},{5,4},{6,5},{7,6},{8,7},{9,8},{10,9},{11,1... | collective-permute-start | bytes 3104 | tf_op jit(solution)/shard_map/ppermute | solution.py:26
  116.6 6.0 collective-permute-start.5
  269.1 12.1 %collective-permute-start.7 = (f32[1,128]{1,0:T(1,128)S(1)}, f32[1,128]{1,0:T(1,128)S(1)}, u32[]{:S(2)}, u32[]{:S(2)}) collective-permute-start(f32[1,128]{1,0:T(1,128)S(1)} %get-tuple-element.43), channel_id=1, source_target_pairs={{0,16},{16,32},{32,48},{48,64},{64,80},{80,96},{96,112},{1,17},{17... | collective-permute-start | bytes 1544 | tf_op jit(solution)/shard_map/ppermute | solution.py:25
  271.5 9.7 %collective-permute-start.6 = (f32[1,128]{1,0:T(1,128)S(1)}, f32[1,128]{1,0:T(1,128)S(1)}, u32[]{:S(2)}, u32[]{:S(2)}) collective-permute-start(f32[1,128]{1,0:T(1,128)S(1)} %get-tuple-element.44), channel_id=1, source_target_pairs={{16,0},{32,16},{48,32},{64,48},{80,64},{96,80},{112,96},{17,1},{33... | collective-permute-start | bytes 1544 | tf_op jit(solution)/shard_map/ppermute | solution.py:26
  274.6 17.2 %all-to-all-start.2 = ((f32[2,256,128]{2,0,1:T(2,128)}), f32[2,256,128]{2,0,1:T(2,128)S(1)}, u32[]{:S(2)}, u32[]{:S(2)}) async-start(f32[2,256,128]{2,0,1:T(2,128)} %copy.54), calls=%async_computation.2 | async-start | bytes 524288 | tf_op jit(solution)/shard_map/all_to_all | solution.py:180
  281.3 7.8 %collective-permute-start.8 = (f32[258,1]{1,0:T(8,128)S(1)}, f32[258,1]{1,0:T(8,128)S(1)}, u32[]{:S(2)}, u32[]{:S(2)}) collective-permute-start(f32[258,1]{1,0:T(8,128)S(1)} %get-tuple-element.37), channel_id=1, source_target_pairs={{1,0},{2,1},{3,2},{4,3},{5,4},{6,5},{7,6},{8,7},{9,8},{10,9},{11,1... | collective-permute-start | bytes 3104 | tf_op jit(solution)/shard_map/ppermute | solution.py:26
  282.6 6.5 %collective-permute-start.9 = (f32[258,1]{1,0:T(8,128)S(1)}, f32[258,1]{1,0:T(8,128)S(1)}, u32[]{:S(2)}, u32[]{:S(2)}) collective-permute-start(f32[258,1]{1,0:T(8,128)S(1)} %get-tuple-element.38), channel_id=1, source_target_pairs={{0,1},{1,2},{2,3},{3,4},{4,5},{5,6},{6,7},{7,8},{8,9},{9,10},{10,1... | collective-permute-start | bytes 3104 | tf_op jit(solution)/shard_map/ppermute | solution.py:25
  436.2 11.4 %collective-permute-start.11 = (f32[1,128]{1,0:T(1,128)S(1)}, f32[1,128]{1,0:T(1,128)S(1)}, u32[]{:S(2)}, u32[]{:S(2)}) collective-permute-start(f32[1,128]{1,0:T(1,128)S(1)} %get-tuple-element.41), channel_id=1, source_target_pairs={{0,16},{16,32},{32,48},{48,64},{64,80},{80,96},{96,112},{1,17},{17... | collective-permute-start | bytes 1544 | tf_op jit(solution)/shard_map/ppermute | solution.py:25
  438.6 8.9 %collective-permute-start.10 = (f32[1,128]{1,0:T(1,128)S(1)}, f32[1,128]{1,0:T(1,128)S(1)}, u32[]{:S(2)}, u32[]{:S(2)}) collective-permute-start(f32[1,128]{1,0:T(1,128)S(1)} %get-tuple-element.42), channel_id=1, source_target_pairs={{16,0},{32,16},{48,32},{64,48},{80,64},{96,80},{112,96},{17,1},{33... | collective-permute-start | bytes 1544 | tf_op jit(solution)/shard_map/ppermute | solution.py:26
  441.8 17.2 %all-to-all-start.3 = ((f32[2,256,128]{2,0,1:T(2,128)}), f32[2,256,128]{2,0,1:T(2,128)S(1)}, u32[]{:S(2)}, u32[]{:S(2)}) async-start(f32[2,256,128]{2,0,1:T(2,128)} %copy.55), calls=%async_computation.3 | async-start | bytes 524288 | tf_op jit(solution)/shard_map/all_to_all | solution.py:180
  447.6 5.4 copy-start.7
  447.7 7.8 %collective-permute-start.12 = (f32[258,1]{1,0:T(8,128)S(1)}, f32[258,1]{1,0:T(8,128)S(1)}, u32[]{:S(2)}, u32[]{:S(2)}) collective-permute-start(f32[258,1]{1,0:T(8,128)S(1)} %get-tuple-element.35), channel_id=1, source_target_pairs={{1,0},{2,1},{3,2},{4,3},{5,4},{6,5},{7,6},{8,7},{9,8},{10,9},{11,1... | collective-permute-start | bytes 3104 | tf_op jit(solution)/shard_map/ppermute | solution.py:26
  449.0 6.5 %collective-permute-start.13 = (f32[258,1]{1,0:T(8,128)S(1)}, f32[258,1]{1,0:T(8,128)S(1)}, u32[]{:S(2)}, u32[]{:S(2)}) collective-permute-start(f32[258,1]{1,0:T(8,128)S(1)} %get-tuple-element.36), channel_id=1, source_target_pairs={{0,1},{1,2},{2,3},{3,4},{4,5},{5,6},{6,7},{7,8},{8,9},{9,10},{10,1... | collective-permute-start | bytes 3104 | tf_op jit(solution)/shard_map/ppermute | solution.py:25
  455.7 3.5 copy-start.9
where the time goes:
time: 606 us; the launch traced here: 604 us
  blocking collectives  462 us (76%)
  starting transfers between devices  64.7 us (11%)
  between operations  24.3 us (4%)
  other arithmetic  19.4 us (3%)
  local copies, waits for them, and re-layouts  14.4 us (2%)
  waiting for transfers between devices  10.5 us (2%)
  matrix products  9.18 us (2%)
    psum x7, blocking collectives, global_dot(): return lax.psum(inner_local(former, latter), ('gx', 'gy'))  462 us
    ppermute x6, starting transfers between devices, extended(): before = lax.ppermute(last, axis, up)  19.5 us
    all_to_all x3, starting transfers between devices, local(): lax.all_to_all(jnp.stack([outgoing, samples]), ('gx', 'gy'), split_axis=1...  17.9 us
  transfers between devices with their start and end apart: 18, of which 4 were waited for; matrix products, arithmetic and copies ran while one was open for 3% of the time, Pallas kernels for 0%

commit v1 on v0

v1 whole, which is shorter than its diff:
```python
import jax
import jax.numpy as jnp
from jax import lax
from jax.experimental import pallas as pl
from jax.experimental.pallas import tpu as pltpu
from jax.sharding import PartitionSpec as P

LOGICAL = pl.DeviceIdType.LOGICAL
F32 = jnp.float32
BF16 = jnp.bfloat16

N = 128
ROWS = 256
BAND = 64
ROWS0 = 9
ROWS1 = 6

HOPS = (0, 1, 2, 1)
OFFSETS = sorted(
    (
        (dy, dc, dz, dx)
        for dy in range(4)
        for dc in range(2)
        for dz in range(4)
        for dx in range(4)
        if (dy, dc, dz, dx) != (0, 0, 0, 0)
    ),
    key=lambda o: (-(2 * (HOPS[o[0]] + HOPS[o[2]] + HOPS[o[3]]) + o[1]), o),
)


def split(value):
    high = value.astype(BF16)
    rest = value - high.astype(F32)
    middle = rest.astype(BF16)
    low = (rest - middle.astype(F32)).astype(BF16)
    return [high, middle, low]


def pick(hot, fields):
    parts = [part for field in fields for part in split(field)]
    out = jnp.dot(hot, jnp.concatenate(parts, axis=1), preferred_element_type=F32)
    n = fields[0].shape[1]
    return [
        out[:, 3 * n * i : 3 * n * i + n]
        + out[:, 3 * n * i + n : 3 * n * i + 2 * n]
        + out[:, 3 * n * i + 2 * n : 3 * n * i + 3 * n]
        for i in range(len(fields))
    ]


def fold(value):
    total = value[0:8]
    for i in range(8, value.shape[0], 8):
        total = total + value[i : i + 8]
    return total


def kernel(
    rhs_m_hbm,
    tx_hbm,
    ty_hbm,
    leak_hbm,
    rhs_f_hbm,
    tf_hbm,
    sf_hbm,
    coef_hbm,
    home_hbm,
    len_hbm,
    mcell_hbm,
    cc_hbm,
    cp_hbm,
    ct_hbm,
    out_m,
    out_f,
    out_l,
    rhs_m,
    tx,
    ty,
    leak,
    rhs_f,
    tf,
    sf,
    coef,
    home,
    blen,
    mcell,
    cc,
    cp,
    ct,
    pm,
    co,
    fm,
    send0,
    recv0,
    send1,
    recv1,
    send2,
    recv2,
    hsend_r,
    hrecv_r,
    hsend_c,
    hrecv_c,
    in_sem,
    ssem,
    rsem,
    hs_sem,
    hr_sem,
):
    gx = lax.axis_index("gx")
    gy = lax.axis_index("gy")
    me = gx * 16 + gy

    pairs = [
        (len_hbm, blen),
        (home_hbm, home),
        (mcell_hbm, mcell),
        (cc_hbm, cc),
        (cp_hbm, cp),
        (ct_hbm, ct),
        (tf_hbm, tf),
        (sf_hbm, sf),
        (rhs_f_hbm, rhs_f),
        (coef_hbm, coef),
        (tx_hbm, tx),
        (ty_hbm, ty),
        (leak_hbm, leak),
        (rhs_m_hbm, rhs_m),
    ]
    loads = [pltpu.make_async_copy(a, b, in_sem.at[i]) for i, (a, b) in enumerate(pairs)]
    for load in loads:
        load.start()

    ys = [lax.rem(gx // 2 + d, 4) * 32 for d in range(4)]
    cs = [lax.rem(gx + d, 2) * 16 for d in range(2)]
    zs = [lax.rem(gy // 4 + d, 4) * 4 for d in range(4)]
    xs = [lax.rem(gy + d, 4) for d in range(4)]

    def target(o):
        return (ys[o[0]] + cs[o[1]]) + (zs[o[2]] + xs[o[3]])

    barrier = pltpu.get_barrier_semaphore()
    for o in OFFSETS:
        pl.semaphore_signal(barrier, inc=1, device_id=target(o), device_id_type=LOGICAL)

    below = lax.rem(gx + 1, 8) * 16 + gy
    above = lax.rem(gx + 7, 8) * 16 + gy
    right = gx * 16 + lax.rem(gy + 1, 16)
    left = gx * 16 + lax.rem(gy + 15, 16)
    has_above = jnp.where(gx > 0, 1.0, 0.0).astype(F32)
    has_below = jnp.where(gx < 7, 1.0, 0.0).astype(F32)
    has_left = jnp.where(gy > 0, 1.0, 0.0).astype(F32)
    has_right = jnp.where(gy < 15, 1.0, 0.0).astype(F32)

    lane = lax.broadcasted_iota(jnp.int32, (N, N), 1)
    row = lax.broadcasted_iota(jnp.int32, (N, N), 0)

    for load in loads[:6]:
        load.wait()
    lanef = lane.astype(F32)
    len_row = blen[...].astype(F32)
    cp_row = cp[...]
    pb_row = cp_row // N
    pc_row = cp_row - pb_row * N
    table = jnp.concatenate(
        [
            len_row,
            cc[...].astype(F32),
            pb_row.astype(F32),
            pc_row.astype(F32),
            ct[...],
            jnp.zeros((N - 9, N), F32),
        ],
        axis=0,
    ).T
    len_col = table[:, 0:1]
    own_hot = [lanef == table[:, 1 + k : 2 + k] for k in range(2)]
    part_rows = [lanef == table[:, 3 + k : 4 + k] for k in range(2)]
    part_hot = [lanef == table[:, 5 + k : 6 + k] for k in range(2)]
    weight = []
    for k in range(2):
        part_len = jnp.sum(jnp.where(part_rows[k], len_row, 0.0), axis=1, keepdims=True)
        live = (table[:, 1 + k : 2 + k] < len_col) & (table[:, 5 + k : 6 + k] < part_len)
        weight.append(jnp.where(live, table[:, 7 + k : 8 + k], 0.0))
    gather_hot = jnp.concatenate([jnp.where(h, 1.0, 0.0) for h in part_rows], axis=0).astype(BF16)
    spread_hot = jnp.concatenate(
        [jnp.where(row == pb_row[k : k + 1], 1.0, 0.0) for k in range(2)], axis=1
    ).astype(BF16)

    def spread(own_values, part_values):
        pieces = jnp.concatenate(
            [jnp.where(part_hot[k], part_values[k], 0.0) for k in range(2)], axis=0
        )
        out = pick(spread_hot, [pieces])[0]
        for k in range(2):
            out = out + jnp.where(own_hot[k], own_values[k], 0.0)
        return out

    for load in loads[6:10]:
        load.wait()
    mask = jnp.where(lanef < len_col, 1.0, 0.0)
    face = jnp.where(lanef + 1.0 < len_col, tf[...], 0.0)
    face_prev = pltpu.roll(face, 1, 1)
    diag_f = sf[...] * mask + face + face_prev + spread(weight, weight)
    safe = diag_f + 1.0 - mask
    inv_f = mask / safe
    metric_l = 1.0 / coef[...] + 1.0 / safe
    inv_l = mask / metric_l
    ratio_l = inv_l / coef[...]
    q0 = inv_f * rhs_f[...]

    def off_f(q):
        rows = pick(gather_hot, [q])[0]
        part = [
            jnp.sum(jnp.where(part_hot[k], rows[k * N : k * N + N], 0.0), axis=1, keepdims=True)
            for k in range(2)
        ]
        own = [jnp.sum(jnp.where(own_hot[k], q, 0.0), axis=1, keepdims=True) for k in range(2)]
        crossing = spread(
            [weight[k] * part[k] for k in range(2)], [weight[k] * own[k] for k in range(2)]
        )
        return face * pltpu.roll(q, N - 1, 1) + face_prev * pltpu.roll(q, 1, 1) + crossing

    q1 = -inv_f * off_f(q0)

    home_hit = row == home[...]
    first = jnp.min(jnp.where(home_hit, lanef, 1e3), axis=1, keepdims=True)
    last = jnp.max(jnp.where(home_hit, lanef, -1.0), axis=1, keepdims=True)
    slots = [
        jnp.where(lanef == first, 1.0, 0.0),
        jnp.where((lanef == last) & (last > first), 1.0, 0.0),
    ]
    mcell_row = mcell[...].astype(F32)
    cells = [jnp.sum(s * mcell_row, axis=1, keepdims=True) for s in slots]
    slot_hot = jnp.concatenate(slots, axis=0).astype(BF16)
    packed = pick(slot_hot, [inv_l, ratio_l, q0, q1])
    for i, value in enumerate(packed):
        send0[:, 2 * i, :] = value[:N]
        send0[:, 2 * i + 1, :] = value[N:]
    send0[:, 8, :] = jnp.where(lane < BAND, cells[0], cells[1])
    recv0[pl.ds(me, 1)] = send0[pl.ds(me, 1)]

    fm[0] = q0
    fm[1] = q1

    for load in loads[10:]:
        load.wait()
    sub8 = lax.broadcasted_iota(jnp.int32, (8, N), 0)
    lane8 = lax.broadcasted_iota(jnp.int32, (8, N), 1)
    ends = jnp.where(
        ((sub8 == 0) & (lane8 == 0)) | ((sub8 == 1) & (lane8 == N - 1)), 1.0, 0.0
    ).astype(BF16)

    def end_cols(field):
        parts = jnp.concatenate(split(field), axis=0)
        out = lax.dot_general(
            ends, parts, (((1,), (1,)), ((), ())), preferred_element_type=F32
        )
        return out[:, :ROWS] + out[:, ROWS : 2 * ROWS] + out[:, 2 * ROWS :]

    def halo_copy(phase, way):
        device = (below, above, right, left)[way]
        send, recv = (hsend_r, hrecv_r) if way < 2 else (hsend_c, hrecv_c)
        return pltpu.make_async_remote_copy(
            send.at[phase, way % 2],
            recv.at[phase, way % 2],
            hs_sem.at[phase, way],
            hr_sem.at[phase, way],
            device_id=device,
            device_id_type=LOGICAL,
        )

    def halo_send(phase, field):
        hsend_r[phase, 0] = field[ROWS - 1 : ROWS]
        hsend_r[phase, 1] = field[0:1]
        cols = end_cols(field)
        hsend_c[phase, 0] = cols[1:2]
        hsend_c[phase, 1] = cols[0:1]
        for way in range(4):
            halo_copy(phase, way).start()

    def wide_cols(before, after):
        both = jnp.concatenate([before, after, jnp.zeros((6, ROWS), F32)], axis=0)
        cols = both.T
        return cols[:, 0:1], cols[:, 1:2]

    row_m = lax.broadcasted_iota(jnp.int32, (ROWS, N), 0)
    lane_m = lax.broadcasted_iota(jnp.int32, (ROWS, N), 1)

    def off_m(p, phase):
        for way in range(4):
            halo_copy(phase, way).wait_recv()
        top = hrecv_r[phase, 0] * has_above
        bottom = hrecv_r[phase, 1] * has_below
        before, after = wide_cols(hrecv_c[phase, 0] * has_left, hrecv_c[phase, 1] * has_right)
        up = jnp.where(row_m == 0, top, pltpu.roll(p, 1, 0))
        down = jnp.where(row_m == ROWS - 1, bottom, pltpu.roll(p, ROWS - 1, 0))
        lft = jnp.where(lane_m == 0, before, pltpu.roll(p, 1, 1))
        rgt = jnp.where(lane_m == N - 1, after, pltpu.roll(p, N - 1, 1))
        return co[0] * down + co[1] * up + co[2] * rgt + co[3] * lft

    hsend_r[0, 0] = tx[ROWS - 1 : ROWS, :]
    hsend_c[0, 0] = end_cols(ty[...])[1:2]

    pl.semaphore_wait(barrier, N - 1)
    halo_copy(0, 0).start()
    halo_copy(0, 2).start()

    def send_to_home(o):
        t = target(o)
        pltpu.make_async_remote_copy(
            send0.at[t],
            recv0.at[me],
            ssem.at[0],
            rsem.at[0],
            device_id=t,
            device_id_type=LOGICAL,
        ).start()

    for o in OFFSETS[:40]:
        send_to_home(o)

    halo_copy(0, 0).wait_recv()
    halo_copy(0, 2).wait_recv()
    tx_prev = jnp.where(row_m == 0, hrecv_r[0, 0] * has_above, pltpu.roll(tx[...], 1, 0))
    left_col, _ = wide_cols(hrecv_c[0, 0] * has_left, jnp.zeros((1, ROWS), F32))
    ty_prev = jnp.where(lane_m == 0, left_col, pltpu.roll(ty[...], 1, 1))
    diag_m = leak[...] + tx[...] + tx_prev + ty[...] + ty_prev
    inv_m = 1.0 / diag_m
    p0 = rhs_m[...] * inv_m
    halo_send(1, p0)
    pm[0] = p0
    co[0] = tx[...] * inv_m
    co[1] = tx_prev * inv_m
    co[2] = ty[...] * inv_m
    co[3] = ty_prev * inv_m
    co[4] = diag_m
    co[5] = inv_m

    for o in OFFSETS[40:80]:
        send_to_home(o)

    p1 = -off_m(pm[0], 1)
    halo_send(2, p1)
    pm[1] = p1

    for o in OFFSETS[80:]:
        send_to_home(o)

    slot_hot_t = jnp.concatenate([s.T for s in slots], axis=1).astype(BF16)
    q2_part = -inv_f * off_f(fm[1])
    pm[2] = -off_m(pm[1], 2)
    dm = co[4]
    moments = [
        fold(dm * pm[0] * pm[0]) + fold(safe * fm[0] * fm[0]),
        fold(dm * pm[0] * pm[1]) + fold(safe * fm[0] * fm[1]),
        fold(dm * pm[1] * pm[1]) + fold(safe * fm[1] * fm[1]),
    ]

    def all_arrived(send, recv, i):
        return pltpu.make_async_remote_copy(
            send.at[pl.ds(0, N - 1)],
            recv.at[pl.ds(0, N - 1)],
            ssem.at[i],
            rsem.at[i],
            device_id=right,
            device_id_type=LOGICAL,
        )

    all_arrived(send0, recv0, 0).wait_recv()
    lane_band = jnp.where(lane < BAND, lane, lane - BAND).astype(F32)
    hit = jnp.where(recv0[:, 8, :] == lane_band, 1.0, 0.0)
    hit_slots = jnp.concatenate(
        [jnp.where(lane < BAND, hit, 0.0), jnp.where(lane < BAND, 0.0, hit)], axis=0
    ).astype(BF16)
    hit_t = hit.T
    hit_rows = jnp.concatenate([hit_t[:BAND], hit_t[BAND:]], axis=1).astype(BF16)

    def sample(fields):
        return pick(hit_slots, [jnp.concatenate([f, f], axis=0) for f in fields])

    p0_at, p1_at = sample([pm[0, 0:BAND], pm[1, 0:BAND]])

    def both(r):
        return jnp.concatenate([recv0[:, r, :], recv0[:, r + 1, :]], axis=0)

    inv_at, ratio_at = both(0), both(2)
    l1 = inv_at * (p0_at - both(4))
    l2 = inv_at * (p1_at - both(6)) - (ratio_at + 1.0) * l1
    pm[2, 0:BAND] += co[5, 0:BAND] * pick(hit_rows, [l1])[0]
    p2 = pm[2]
    halo_send(3, p2)
    p2_at = sample([p2[0:BAND]])[0]
    for i, value in enumerate((l1, l2, p2_at)):
        send1[:, 2 * i, :] = value[:N]
        send1[:, 2 * i + 1, :] = value[N:]
    recv1[pl.ds(me, 1)] = send1[pl.ds(me, 1)]
    for o in OFFSETS:
        t = target(o)
        pltpu.make_async_remote_copy(
            send1.at[t],
            recv1.at[me],
            ssem.at[1],
            rsem.at[1],
            device_id=t,
            device_id_type=LOGICAL,
        ).start()
    pm[3] = -off_m(pm[2], 3)
    pm[3, 0:BAND] += co[5, 0:BAND] * pick(hit_rows, [l2])[0]
    d2 = co[4] * pm[2]
    moments.append(fold(d2 * pm[1]))
    moments.append(fold(d2 * pm[2]))
    moments.append(fold(d2 * pm[3]))
    moments.append(fold(co[4] * pm[3] * pm[3]))

    all_arrived(send1, recv1, 1).wait_recv()

    def returned(r):
        return jnp.concatenate([recv1[:, r, :], recv1[:, r + 1, :]], axis=0)

    l1, l2, p2_at = pick(slot_hot_t, [returned(0), returned(2), returned(4)])
    q2 = q2_part - inv_f * l1
    q3 = -inv_f * (off_f(q2) + l2)
    l3 = inv_l * (p2_at - q2) - (ratio_l + 1.0) * l2
    fm[2] = q2
    fm[3] = l1
    fm[4] = l2
    m1, m2 = metric_l * l1, metric_l * l2
    s2 = safe * q2
    moments[2] += fold(m1 * l1)
    moments[3] += fold(s2 * fm[1] + m1 * l2)
    moments[4] += fold(s2 * q2 + m2 * l2)
    moments[5] += fold(s2 * q3 + m2 * l3)
    moments[6] += fold(safe * q3 * q3 + metric_l * l3 * l3)
    rows = [jnp.sum(m, axis=0, keepdims=True) for m in moments]
    sums = jnp.sum(jnp.concatenate(rows + [jnp.zeros((1, N), F32)], axis=0), axis=1, keepdims=True)
    mine = jnp.sum(jnp.where(lane8 == sub8, sums, 0.0), axis=0, keepdims=True)
    send2[...] = mine
    recv2[pl.ds(me, 1)] = mine[None]
    for o in OFFSETS:
        pltpu.make_async_remote_copy(
            send2,
            recv2.at[me],
            ssem.at[2],
            rsem.at[2],
            device_id=target(o),
            device_id_type=LOGICAL,
        ).start()
    all_arrived(recv2, recv2, 2).wait_recv()
    total = jnp.sum(recv2[...], axis=0)
    mu = [jnp.broadcast_to(total[:, i : i + 1], (1, N)) for i in range(7)]

    n0 = mu[0]
    a0 = mu[1] / n0
    n1 = mu[2] - a0 * mu[1]
    a1 = (mu[3] - a0 * (mu[2] + n1)) / n1
    b1 = n1 / n0
    c1 = -(a0 + a1)
    c0 = a0 * a1 - b1
    n2 = mu[4] + c1 * mu[3] + c0 * mu[2]
    a2 = (mu[5] + c1 * mu[4] + c0 * mu[3]) / n2 + c1
    b2 = n2 / n1
    square = mu[6] + 2.0 * c1 * mu[5] + (c1 * c1 + 2.0 * c0) * mu[4] + 2.0 * c0 * c1 * mu[3] + c0 * c0 * mu[2]
    n3 = square - (a2 * a2 + b2) * n2
    gammas = [jnp.sqrt(n0), jnp.sqrt(b1), jnp.sqrt(b2), jnp.sqrt(n3 / n2)]
    curvatures = [a0 + 1.0, a1 + 1.0, a2 + 1.0]
    i0, i1, i2 = lax.rsqrt(n0), lax.rsqrt(n1), lax.rsqrt(n2)
    zero = jnp.zeros_like(n0)
    one = jnp.ones_like(n0)
    basis = [(i0, zero, zero), (-a0 * i1, i1, zero), (c0 * i2, c1 * i2, i2)]
    cos_old, cos_now, sin_old, sin_now = one, one, zero, zero
    rhs_scale = gammas[0]
    search_old = search_now = iterate = (zero, zero, zero)
    for k in range(3):
        gamma, gamma_new = gammas[k], gammas[k + 1]
        alpha_zero = cos_now * curvatures[k] - cos_old * sin_now * gamma
        alpha_one = jnp.sqrt(alpha_zero * alpha_zero + gamma_new * gamma_new)
        alpha_two = sin_now * curvatures[k] + cos_old * cos_now * gamma
        alpha_three = sin_old * gamma
        cos_new, sin_new = alpha_zero / alpha_one, gamma_new / alpha_one
        search_new = tuple(
            (z - alpha_three * old - alpha_two * now) / alpha_one
            for z, old, now in zip(basis[k], search_old, search_now)
        )
        iterate = tuple(x + cos_new * rhs_scale * w for x, w in zip(iterate, search_new))
        rhs_scale = -sin_new * rhs_scale
        cos_old, cos_now, sin_old, sin_now = cos_now, cos_new, sin_now, sin_new
        search_old, search_now = search_now, search_new
    x0, x1, x2 = iterate
    out_m[...] = x0 * pm[0] + x1 * pm[1] + x2 * pm[2]
    out_f[...] = x0 * fm[0] + x1 * fm[1] + x2 * fm[2]
    out_l[...] = x1 * fm[3] + x2 * fm[4]

    all_arrived(send0, recv0, 0).wait_send()
    all_arrived(send1, recv1, 1).wait_send()
    all_arrived(recv2, recv2, 2).wait_send()
    halo_copy(0, 0).wait_send()
    halo_copy(0, 2).wait_send()
    for phase in range(1, 4):
        for way in range(4):
            halo_copy(phase, way).wait_send()


def local(
    rhs_matrix,
    trans_x,
    trans_y,
    leak_matrix,
    rhs_fracture,
    trans_frac,
    store_frac,
    mortar_coef,
    block_home,
    block_len,
    mortar_cell,
    cross_cell,
    cross_partner,
    cross_trans,
):
    tile, block = (ROWS, N), (N, N)
    vmem = lambda shape, kind=F32: pltpu.VMEM(shape, kind)
    return pl.pallas_call(
        kernel,
        out_shape=(
            jax.ShapeDtypeStruct(tile, F32),
            jax.ShapeDtypeStruct(block, F32),
            jax.ShapeDtypeStruct(block, F32),
        ),
        in_specs=[pl.BlockSpec(memory_space=pl.ANY)] * 14,
        out_specs=(pl.BlockSpec(memory_space=pltpu.VMEM),) * 3,
        scratch_shapes=[vmem(tile)] * 4
        + [vmem(block)] * 4
        + [vmem((1, N), jnp.int32)] * 3
        + [vmem((2, N), jnp.int32)] * 2
        + [vmem((2, N))]
        + [
            vmem((4,) + tile),
            vmem((6,) + tile),
            vmem((5,) + block),
            vmem((N, ROWS0, N)),
            vmem((N, ROWS0, N)),
            vmem((N, ROWS1, N)),
            vmem((N, ROWS1, N)),
            vmem((1, N)),
            vmem((N, 1, N)),
            vmem((4, 2, 1, N)),
            vmem((4, 2, 1, N)),
            vmem((4, 2, 1, ROWS)),
            vmem((4, 2, 1, ROWS)),
            pltpu.SemaphoreType.DMA((14,)),
            pltpu.SemaphoreType.DMA((3,)),
            pltpu.SemaphoreType.DMA((3,)),
            pltpu.SemaphoreType.DMA((4, 4)),
            pltpu.SemaphoreType.DMA((4, 4)),
        ],
        compiler_params=pltpu.CompilerParams(
            collective_id=0, has_side_effects=True, vmem_limit_bytes=40 * 2**20
        ),
    )(
        rhs_matrix,
        trans_x,
        trans_y,
        leak_matrix,
        rhs_fracture,
        trans_frac,
        store_frac,
        mortar_coef,
        block_home.T,
        block_len.reshape(1, N),
        mortar_cell.T,
        cross_cell.T,
        cross_partner.T,
        cross_trans.T,
    )


def solution(mesh):
    tiles, blocks = P("gx", "gy"), P(("gx", "gy"), None)
    return jax.shard_map(
        local,
        mesh=mesh,
        in_specs=(tiles,) * 4 + (blocks,) * 5 + (P(("gx", "gy")),) + (blocks,) * 4,
        out_specs=(tiles, blocks, blocks),
        check_vma=False,
    )
```

time: 606 us -> 51.1 us (0.08)
  blocking collectives: 462 us -> 0 us
  starting transfers between devices: 64.7 us -> 0 us
  Pallas kernels: 0 us -> 40.4 us
  between operations: 24.3 us -> 0.7 us
  other arithmetic: 19.4 us -> 0 us
  waiting for transfers between devices: 10.5 us -> 0 us
  matrix products: 9.18 us -> 0 us
    psum x7 -> x0, blocking collectives: 462 us -> none  [global_dot(): return lax.psum(inner_local(former, latter), ('gx', 'gy'))]
    pallas_call x0 -> x1, Pallas kernels: none -> 40.4 us  [local(): pl.pallas_call(kernel, out_shape=(jax.ShapeDtypeStruct(tile, F32), jax.Sh...]
    ppermute x14 -> x0, starting transfers between devices: 37 us -> none  [the longest x6 19.5 us: extended(): before = lax.ppermute(last, axis, up)]
    all_to_all x4 -> x0, starting transfers between devices: 27.7 us -> none  [the longest x3 17.9 us: local(): lax.all_to_all(jnp.stack([outgoing, samples]), ('gx', 'gy'), split_axis=1...]
    reduce_sum x26 -> x0, other arithmetic: 14.6 us -> none  [the longest x7 4.55 us: inner_local(): jnp.sum(former[0] * latter[0]) + jnp.sum(former[1] * latter[1])]
    all_to_all x4 -> x0, waiting for transfers between devices: 9.52 us -> none  [the longest x3 9.52 us: local(): lax.all_to_all(jnp.stack([outgoing, samples]), ('gx', 'gy'), split_axis=1...]
    dot_general x16 -> x0, matrix products: 9.18 us -> none  [the longest x4 4.08 us: spread_cross(): jnp.dot(partner_rows.T, pieces, precision=highest, preferred_element_type...]
    unnamed x30 -> x31, local copies, waits for them, and re-layouts: 3.42 us -> 9.58 us
  transfers between devices with their start and end apart: 18 -> 0, of which waited for: 4 -> 0; matrix products, arithmetic and copies ran while one was open for 3% -> 0% of each run, Pallas kernels for 0% -> 0%
where the time goes in v1:
time: 51.1 us; the launch traced here: 50.7 us
  Pallas kernels  40.4 us (79%)
  local copies, waits for them, and re-layouts  9.58 us (19%)
  between operations  0.7 us (1%)
    pallas_call x1, Pallas kernels, local(): pl.pallas_call(kernel, out_shape=(jax.ShapeDtypeStruct(tile, F32), jax.Sh...  40.4 us
    unnamed x31, local copies, waits for them, and re-layouts  9.58 us

profile of v1, /device:TPU:1, one launch (start us, length us, event | category | flops | bytes accessed | tf_op | source)
XLA Modules:
  0.0 50.7 jit_solution(4683692617892758674)
XLA Ops:
  0.6 0.0 copy-start.12
  0.6 0.0 copy-start.13
  0.7 0.0 copy-start.9
  0.7 0.0 copy-start.10
  0.7 0.0 copy-start.8
  0.7 0.0 copy-start.11
  0.7 0.6 %copy-done.12 = s32[128]{0:T(128)S(1)} copy-done((s32[128]{0:T(128)S(1)}, s32[128]{0:T(128)}, u32[]{:S(2)}) %copy-start.12) | copy-done | bytes 536
  1.3 0.0 copy-done.13
  1.3 0.0 copy-done.9
  1.3 0.0 copy-done.10
  1.4 0.0 copy-done.8
  1.4 0.0 copy-done.11
  1.4 0.0 copy-start
  1.4 0.9 %copy-done = f32[256,128]{1,0:T(8,128)S(1)} copy-done((f32[256,128]{1,0:T(8,128)S(1)}, f32[256,128]{1,0:T(8,128)}, u32[]{:S(2)}) %copy-start) | copy-done | bytes 131096
  2.3 0.0 copy-start.1
  2.3 0.9 %copy-done.1 = f32[256,128]{1,0:T(8,128)S(1)} copy-done((f32[256,128]{1,0:T(8,128)S(1)}, f32[256,128]{1,0:T(8,128)}, u32[]{:S(2)}) %copy-start.1) | copy-done | bytes 131096
  3.2 0.0 copy-start.2
  3.2 0.9 %copy-done.2 = f32[256,128]{1,0:T(8,128)S(1)} copy-done((f32[256,128]{1,0:T(8,128)S(1)}, f32[256,128]{1,0:T(8,128)}, u32[]{:S(2)}) %copy-start.2) | copy-done | bytes 131096
  4.1 0.0 copy-start.3
  4.1 0.9 %copy-done.3 = f32[256,128]{1,0:T(8,128)S(1)} copy-done((f32[256,128]{1,0:T(8,128)S(1)}, f32[256,128]{1,0:T(8,128)}, u32[]{:S(2)}) %copy-start.3) | copy-done | bytes 131096
  5.0 0.0 copy-start.4
  5.0 0.8 %copy-done.4 = f32[128,128]{1,0:T(8,128)S(1)} copy-done((f32[128,128]{1,0:T(8,128)S(1)}, f32[128,128]{1,0:T(8,128)}, u32[]{:S(2)}) %copy-start.4) | copy-done | bytes 65560
  5.8 0.0 copy-start.5
  5.8 0.8 %copy-done.5 = f32[128,128]{1,0:T(8,128)S(1)} copy-done((f32[128,128]{1,0:T(8,128)S(1)}, f32[128,128]{1,0:T(8,128)}, u32[]{:S(2)}) %copy-start.5) | copy-done | bytes 65560
  6.7 0.0 copy-start.6
  6.7 0.8 %copy-done.6 = f32[128,128]{1,0:T(8,128)S(1)} copy-done((f32[128,128]{1,0:T(8,128)S(1)}, f32[128,128]{1,0:T(8,128)}, u32[]{:S(2)}) %copy-start.6) | copy-done | bytes 65560
  7.5 0.0 copy-start.7
  7.5 0.8 %copy-done.7 = f32[128,128]{1,0:T(8,128)S(1)} copy-done((f32[128,128]{1,0:T(8,128)S(1)}, f32[128,128]{1,0:T(8,128)}, u32[]{:S(2)}) %copy-start.7) | copy-done | bytes 65560
  8.4 40.4 %shard_map.157 = (f32[256,128]{1,0:T(8,128)S(1)}, f32[128,128]{1,0:T(8,128)S(1)}, f32[128,128]{1,0:T(8,128)S(1)}) custom-call(f32[256,128]{1,0:T(8,128)S(1)} %copy-done, f32[256,128]{1,0:T(8,128)S(1)} %copy-done.1, f32[256,128]{1,0:T(8,128)S(1)} %copy-done.2, f32[256,128]{1,0:T(8,128)S(1)} %copy-done.3, f32[128,128]{1,0:T(8,128)S(1)} %copy-done.4, ...), custom_call_target="tpu_custom_call" | custom-call | tf_op jit(solution)/shard_map/pallas_call | solution.py:522
  48.8 0.7 %copy.20 = f32[256,128]{1,0:T(8,128)} copy(f32[256,128]{1,0:T(8,128)S(1)} %get-tuple-element.6) | data formatting | bytes 262144
  49.4 0.6 %copy.21 = f32[128,128]{1,0:T(8,128)} copy(f32[128,128]{1,0:T(8,128)S(1)} %get-tuple-element.7) | data formatting | bytes 131072
  50.0 0.6 %copy.22 = f32[128,128]{1,0:T(8,128)} copy(f32[128,128]{1,0:T(8,128)S(1)} %get-tuple-element.8) | data formatting | bytes 131072
Async XLA Ops:
  0.6 0.7 %copy-start.12 = (s32[128]{0:T(128)S(1)}, s32[128]{0:T(128)}, u32[]{:S(2)}) copy-start(s32[128]{0:T(128)} %param.23) | copy-start | bytes 1540
  0.6 0.7 %copy-start.13 = (s32[128,1]{0,1:T(1,128)S(1)}, s32[128,1]{0,1:T(1,128)}, u32[]{:S(2)}) copy-start(s32[128,1]{0,1:T(1,128)} %param.24) | copy-start | bytes 1540
  0.7 0.7 %copy-start.9 = (s32[128,2]{0,1:T(2,128)S(1)}, s32[128,2]{0,1:T(2,128)}, u32[]{:S(2)}) copy-start(s32[128,2]{0,1:T(2,128)} %param.26) | copy-start | bytes 3076
  0.7 0.7 %copy-start.10 = (f32[128,2]{0,1:T(2,128)S(1)}, f32[128,2]{0,1:T(2,128)}, u32[]{:S(2)}) copy-start(f32[128,2]{0,1:T(2,128)} %param.27) | copy-start | bytes 3076
  0.7 0.7 %copy-start.8 = (s32[128,2]{0,1:T(2,128)S(1)}, s32[128,2]{0,1:T(2,128)}, u32[]{:S(2)}) copy-start(s32[128,2]{0,1:T(2,128)} %param.25) | copy-start | bytes 3076
  0.7 0.7 %copy-start.11 = (s32[128,1]{0,1:T(1,128)S(1)}, s32[128,1]{0,1:T(1,128)}, u32[]{:S(2)}) copy-start(s32[128,1]{0,1:T(1,128)} %param.22) | copy-start | bytes 1540
  1.4 0.9 %copy-start = (f32[256,128]{1,0:T(8,128)S(1)}, f32[256,128]{1,0:T(8,128)}, u32[]{:S(2)}) copy-start(f32[256,128]{1,0:T(8,128)} %rhs_m_hbm.1) | copy-start | bytes 393220
  2.3 0.9 %copy-start.1 = (f32[256,128]{1,0:T(8,128)S(1)}, f32[256,128]{1,0:T(8,128)}, u32[]{:S(2)}) copy-start(f32[256,128]{1,0:T(8,128)} %tx_hbm.1) | copy-start | bytes 393220
  3.2 0.9 %copy-start.2 = (f32[256,128]{1,0:T(8,128)S(1)}, f32[256,128]{1,0:T(8,128)}, u32[]{:S(2)}) copy-start(f32[256,128]{1,0:T(8,128)} %ty_hbm.1) | copy-start | bytes 393220
  4.1 0.9 %copy-start.3 = (f32[256,128]{1,0:T(8,128)S(1)}, f32[256,128]{1,0:T(8,128)}, u32[]{:S(2)}) copy-start(f32[256,128]{1,0:T(8,128)} %leak_hbm.1) | copy-start | bytes 393220
  5.0 0.8 %copy-start.4 = (f32[128,128]{1,0:T(8,128)S(1)}, f32[128,128]{1,0:T(8,128)}, u32[]{:S(2)}) copy-start(f32[128,128]{1,0:T(8,128)} %rhs_f_hbm.1) | copy-start | bytes 196612
  5.8 0.8 %copy-start.5 = (f32[128,128]{1,0:T(8,128)S(1)}, f32[128,128]{1,0:T(8,128)}, u32[]{:S(2)}) copy-start(f32[128,128]{1,0:T(8,128)} %tf_hbm.1) | copy-start | bytes 196612
  6.7 0.8 %copy-start.6 = (f32[128,128]{1,0:T(8,128)S(1)}, f32[128,128]{1,0:T(8,128)}, u32[]{:S(2)}) copy-start(f32[128,128]{1,0:T(8,128)} %sf_hbm.1) | copy-start | bytes 196612
  7.5 0.8 %copy-start.7 = (f32[128,128]{1,0:T(8,128)S(1)}, f32[128,128]{1,0:T(8,128)}, u32[]{:S(2)}) copy-start(f32[128,128]{1,0:T(8,128)} %coef_hbm.1) | copy-start | bytes 196612

commit v2 on v1

--- a/solution.py
+++ b/solution.py
@@ -14,6 +14,8 @@
 BAND = 64
 ROWS0 = 9
 ROWS1 = 6
+
+FIRST = 100
 
 HOPS = (0, 1, 2, 1)
 OFFSETS = sorted(
@@ -71,9 +73,9 @@
     cc_hbm,
     cp_hbm,
     ct_hbm,
-    out_m,
-    out_f,
-    out_l,
+    pm,
+    fm,
+    factors,
     rhs_m,
     tx,
     ty,
@@ -88,9 +90,8 @@
     cc,
     cp,
     ct,
-    pm,
+    p3_ref,
     co,
-    fm,
     send0,
     recv0,
     send1,
@@ -101,11 +102,17 @@
     hrecv_r,
     hsend_c,
     hrecv_c,
+    esend_r,
+    erecv_r,
+    esend_c,
+    erecv_c,
     in_sem,
     ssem,
     rsem,
     hs_sem,
     hr_sem,
+    es_sem,
+    er_sem,
 ):
     gx = lax.axis_index("gx")
     gy = lax.axis_index("gy")
@@ -147,6 +154,9 @@
     above = lax.rem(gx + 7, 8) * 16 + gy
     right = gx * 16 + lax.rem(gy + 1, 16)
     left = gx * 16 + lax.rem(gy + 15, 16)
+    below_right = lax.rem(gx + 1, 8) * 16 + lax.rem(gy + 1, 16)
+    above_right = lax.rem(gx + 7, 8) * 16 + lax.rem(gy + 1, 16)
+    below_left = lax.rem(gx + 1, 8) * 16 + lax.rem(gy + 15, 16)
     has_above = jnp.where(gx > 0, 1.0, 0.0).astype(F32)
     has_below = jnp.where(gx < 7, 1.0, 0.0).astype(F32)
     has_left = jnp.where(gy > 0, 1.0, 0.0).astype(F32)
@@ -251,12 +261,11 @@
         ((sub8 == 0) & (lane8 == 0)) | ((sub8 == 1) & (lane8 == N - 1)), 1.0, 0.0
     ).astype(BF16)
 
-    def end_cols(field):
-        parts = jnp.concatenate(split(field), axis=0)
-        out = lax.dot_general(
-            ends, parts, (((1,), (1,)), ((), ())), preferred_element_type=F32
-        )
-        return out[:, :ROWS] + out[:, ROWS : 2 * ROWS] + out[:, 2 * ROWS :]
+    def end_cols(fields):
+        parts = jnp.concatenate([part for field in fields for part in split(field)], axis=0)
+        out = lax.dot_general(ends, parts, (((1,), (1,)), ((), ())), preferred_element_type=F32)
+        pieces = [out[:, ROWS * k : ROWS * (k + 1)] for k in range(3 * len(fields))]
+        return [pieces[3 * k] + pieces[3 * k + 1] + pieces[3 * k + 2] for k in range(len(fields))]
 
     def halo_copy(phase, way):
         device = (below, above, right, left)[way]
@@ -273,38 +282,73 @@
     def halo_send(phase, field):
         hsend_r[phase, 0] = field[ROWS - 1 : ROWS]
         hsend_r[phase, 1] = field[0:1]
-        cols = end_cols(field)
+        cols = end_cols([field])[0]
         hsend_c[phase, 0] = cols[1:2]
         hsend_c[phase, 1] = cols[0:1]
         for way in range(4):
             halo_copy(phase, way).start()
 
-    def wide_cols(before, after):
-        both = jnp.concatenate([before, after, jnp.zeros((6, ROWS), F32)], axis=0)
-        cols = both.T
-        return cols[:, 0:1], cols[:, 1:2]
+    def as_cols(rows):
+        cols = jnp.concatenate(rows + [jnp.zeros((8 - len(rows), ROWS), F32)], axis=0).T
+        return [cols[:, k : k + 1] for k in range(len(rows))]
 
     row_m = lax.broadcasted_iota(jnp.int32, (ROWS, N), 0)
     lane_m = lax.broadcasted_iota(jnp.int32, (ROWS, N), 1)
 
-    def off_m(p, phase):
-        for way in range(4):
-            halo_copy(phase, way).wait_recv()
-        top = hrecv_r[phase, 0] * has_above
-        bottom = hrecv_r[phase, 1] * has_below
-        before, after = wide_cols(hrecv_c[phase, 0] * has_left, hrecv_c[phase, 1] * has_right)
+    def off_m(p, top, bottom, before, after):
         up = jnp.where(row_m == 0, top, pltpu.roll(p, 1, 0))
         down = jnp.where(row_m == ROWS - 1, bottom, pltpu.roll(p, ROWS - 1, 0))
         lft = jnp.where(lane_m == 0, before, pltpu.roll(p, 1, 1))
         rgt = jnp.where(lane_m == N - 1, after, pltpu.roll(p, N - 1, 1))
         return co[0] * down + co[1] * up + co[2] * rgt + co[3] * lft
 
-    hsend_r[0, 0] = tx[ROWS - 1 : ROWS, :]
-    hsend_c[0, 0] = end_cols(ty[...])[1:2]
+    def halo(phase):
+        for way in range(4):
+            halo_copy(phase, way).wait_recv()
+        before, after = as_cols([hrecv_c[phase, 0] * has_left, hrecv_c[phase, 1] * has_right])
+        return hrecv_r[phase, 0] * has_above, hrecv_r[phase, 1] * has_below, before, after
+
+    tx_up = jnp.where(row_m == 0, 0.0, pltpu.roll(tx[...], 1, 0))
+    ty_left = jnp.where(lane_m == 0, 0.0, pltpu.roll(ty[...], 1, 1))
+    partial = leak[...] + tx[...] + tx_up + ty[...] + ty_left
+    esend_r[0] = tx[ROWS - 1 : ROWS]
+    esend_r[1] = rhs_m[ROWS - 1 : ROWS]
+    esend_r[2] = partial[ROWS - 1 : ROWS]
+    esend_r[3] = rhs_m[0:1]
+    esend_r[4] = partial[0:1]
+    esend_r[5] = tx[ROWS - 1 : ROWS]
+    esend_r[6] = ty[ROWS - 1 : ROWS]
+    esend_r[7] = ty[0:1]
+    esend_r[8] = tx[ROWS - 1 : ROWS]
+    ty_cols, rhs_cols, partial_cols = end_cols([ty[...], rhs_m[...], partial])
+    esend_c[0] = ty_cols[1:2]
+    esend_c[1] = rhs_cols[1:2]
+    esend_c[2] = partial_cols[1:2]
+    esend_c[3] = rhs_cols[0:1]
+    esend_c[4] = partial_cols[0:1]
+
+    def edge_copy(i):
+        send, recv, start, count, device = (
+            (esend_r, erecv_r, 0, 3, below),
+            (esend_r, erecv_r, 3, 2, above),
+            (esend_r, erecv_r, 5, 2, below_right),
+            (esend_r, erecv_r, 7, 1, above_right),
+            (esend_r, erecv_r, 8, 1, below_left),
+            (esend_c, erecv_c, 0, 3, right),
+            (esend_c, erecv_c, 3, 2, left),
+        )[i]
+        return pltpu.make_async_remote_copy(
+            send.at[pl.ds(start, count)],
+            recv.at[pl.ds(start, count)],
+            es_sem.at[i],
+            er_sem.at[i],
+            device_id=device,
+            device_id_type=LOGICAL,
+        )
 
     pl.semaphore_wait(barrier, N - 1)
-    halo_copy(0, 0).start()
-    halo_copy(0, 2).start()
+    for i in range(7):
+        edge_copy(i).start()
 
     def send_to_home(o):
         t = target(o)
@@ -317,39 +361,53 @@
             device_id_type=LOGICAL,
         ).start()
 
-    for o in OFFSETS[:40]:
+    for o in OFFSETS[:FIRST]:
         send_to_home(o)
 
-    halo_copy(0, 0).wait_recv()
-    halo_copy(0, 2).wait_recv()
-    tx_prev = jnp.where(row_m == 0, hrecv_r[0, 0] * has_above, pltpu.roll(tx[...], 1, 0))
-    left_col, _ = wide_cols(hrecv_c[0, 0] * has_left, jnp.zeros((1, ROWS), F32))
-    ty_prev = jnp.where(lane_m == 0, left_col, pltpu.roll(ty[...], 1, 1))
+    for i in range(7):
+        edge_copy(i).wait_recv()
+    lane_1 = lax.broadcasted_iota(jnp.int32, (1, N), 1)
+
+    def corner(value, factor):
+        return jnp.where(lane_1 == 0, value, 0.0) * factor
+
+    def corner_col(value, factor):
+        return jnp.concatenate([corner(value, factor), jnp.zeros((1, N), F32)], axis=1)
+
+    diag_above = erecv_r[2] + corner(pltpu.roll(erecv_r[6], 1, 1), has_left)
+    diag_below = erecv_r[4] + tx[ROWS - 1 : ROWS] + corner(pltpu.roll(erecv_r[7], 1, 1), has_left)
+    diag_left = erecv_c[2] + corner_col(pltpu.roll(erecv_r[5], 1, 1), has_above)
+    diag_right = erecv_c[4] + esend_c[0] + corner_col(erecv_r[8], has_above)
+    p0_above = erecv_r[1] / diag_above * has_above
+    p0_below = erecv_r[3] / diag_below * has_below
+    ty_col, p0_left, p0_right = as_cols(
+        [
+            erecv_c[0] * has_left,
+            erecv_c[1] / diag_left * has_left,
+            erecv_c[3] / diag_right * has_right,
+        ]
+    )
+    tx_prev = jnp.where(row_m == 0, erecv_r[0] * has_above, pltpu.roll(tx[...], 1, 0))
+    ty_prev = jnp.where(lane_m == 0, ty_col, pltpu.roll(ty[...], 1, 1))
     diag_m = leak[...] + tx[...] + tx_prev + ty[...] + ty_prev
     inv_m = 1.0 / diag_m
-    p0 = rhs_m[...] * inv_m
-    halo_send(1, p0)
-    pm[0] = p0
+    pm[0] = rhs_m[...] * inv_m
     co[0] = tx[...] * inv_m
     co[1] = tx_prev * inv_m
     co[2] = ty[...] * inv_m
     co[3] = ty_prev * inv_m
     co[4] = diag_m
     co[5] = inv_m
-
-    for o in OFFSETS[40:80]:
-        send_to_home(o)
-
-    p1 = -off_m(pm[0], 1)
-    halo_send(2, p1)
+    p1 = -off_m(pm[0], p0_above, p0_below, p0_left, p0_right)
+    halo_send(0, p1)
     pm[1] = p1
 
-    for o in OFFSETS[80:]:
+    for o in OFFSETS[FIRST:]:
         send_to_home(o)
 
     slot_hot_t = jnp.concatenate([s.T for s in slots], axis=1).astype(BF16)
     q2_part = -inv_f * off_f(fm[1])
-    pm[2] = -off_m(pm[1], 2)
+    pm[2] = -off_m(pm[1], *halo(0))
     dm = co[4]
     moments = [
         fold(dm * pm[0] * pm[0]) + fold(safe * fm[0] * fm[0]),
@@ -389,7 +447,7 @@
     l2 = inv_at * (p1_at - both(6)) - (ratio_at + 1.0) * l1
     pm[2, 0:BAND] += co[5, 0:BAND] * pick(hit_rows, [l1])[0]
     p2 = pm[2]
-    halo_send(3, p2)
+    halo_send(1, p2)
     p2_at = sample([p2[0:BAND]])[0]
     for i, value in enumerate((l1, l2, p2_at)):
         send1[:, 2 * i, :] = value[:N]
@@ -405,13 +463,14 @@
             device_id=t,
             device_id_type=LOGICAL,
         ).start()
-    pm[3] = -off_m(pm[2], 3)
-    pm[3, 0:BAND] += co[5, 0:BAND] * pick(hit_rows, [l2])[0]
+    p3_ref[...] = -off_m(pm[2], *halo(1))
+    p3_ref[0:BAND] += co[5, 0:BAND] * pick(hit_rows, [l2])[0]
     d2 = co[4] * pm[2]
     moments.append(fold(d2 * pm[1]))
     moments.append(fold(d2 * pm[2]))
-    moments.append(fold(d2 * pm[3]))
-    moments.append(fold(co[4] * pm[3] * pm[3]))
+    p3 = p3_ref[...]
+    moments.append(fold(d2 * p3))
+    moments.append(fold(co[4] * p3 * p3))
 
     all_arrived(send1, recv1, 1).wait_recv()
 
@@ -486,19 +545,33 @@
         rhs_scale = -sin_new * rhs_scale
         cos_old, cos_now, sin_old, sin_now = cos_now, cos_new, sin_now, sin_new
         search_old, search_now = search_now, search_new
-    x0, x1, x2 = iterate
-    out_m[...] = x0 * pm[0] + x1 * pm[1] + x2 * pm[2]
-    out_f[...] = x0 * fm[0] + x1 * fm[1] + x2 * fm[2]
-    out_l[...] = x1 * fm[3] + x2 * fm[4]
+    factors[...] = jnp.concatenate(list(iterate) + [zero] * 5, axis=0)
 
     all_arrived(send0, recv0, 0).wait_send()
     all_arrived(send1, recv1, 1).wait_send()
     all_arrived(recv2, recv2, 2).wait_send()
-    halo_copy(0, 0).wait_send()
-    halo_copy(0, 2).wait_send()
-    for phase in range(1, 4):
+    for i in range(7):
+        edge_copy(i).wait_send()
+    for phase in range(2):
         for way in range(4):
             halo_copy(phase, way).wait_send()
+
+
+def combine(pm, fm, factors, out_m, out_f, out_l, om, of, ol, sem):
+    x0, x1, x2 = factors[0:1], factors[1:2], factors[2:3]
+    stores = [
+        pltpu.make_async_copy(om, out_m, sem.at[0]),
+        pltpu.make_async_copy(of, out_f, sem.at[1]),
+        pltpu.make_async_copy(ol, out_l, sem.at[2]),
+    ]
+    om[...] = x0 * pm[0] + x1 * pm[1] + x2 * pm[2]
+    stores[0].start()
+    of[...] = x0 * fm[0] + x1 * fm[1] + x2 * fm[2]
+    stores[1].start()
+    ol[...] = x1 * fm[3] + x2 * fm[4]
+    stores[2].start()
+    for store in stores:
+        store.wait()
 
 
 def local(
@@ -519,13 +592,9 @@
 ):
     tile, block = (ROWS, N), (N, N)
     vmem = lambda shape, kind=F32: pltpu.VMEM(shape, kind)
-    return pl.pallas_call(
+    results = pl.pallas_call(
         kernel,
-        out_shape=(
-            jax.ShapeDtypeStruct(tile, F32),
-            jax.ShapeDtypeStruct(block, F32),
-            jax.ShapeDtypeStruct(block, F32),
-        ),
+        out_shape=(vmem((3,) + tile), vmem((5,) + block), vmem((8, N))),
         in_specs=[pl.BlockSpec(memory_space=pl.ANY)] * 14,
         out_specs=(pl.BlockSpec(memory_space=pltpu.VMEM),) * 3,
         scratch_shapes=[vmem(tile)] * 4
@@ -534,44 +603,65 @@
         + [vmem((2, N), jnp.int32)] * 2
         + [vmem((2, N))]
         + [
-            vmem((4,) + tile),
+            vmem(tile),
             vmem((6,) + tile),
-            vmem((5,) + block),
             vmem((N, ROWS0, N)),
             vmem((N, ROWS0, N)),
             vmem((N, ROWS1, N)),
             vmem((N, ROWS1, N)),
             vmem((1, N)),
             vmem((N, 1, N)),
-            vmem((4, 2, 1, N)),
-            vmem((4, 2, 1, N)),
-            vmem((4, 2, 1, ROWS)),
-            vmem((4, 2, 1, ROWS)),
+            vmem((2, 2, 1, N)),
+            vmem((2, 2, 1, N)),
+            vmem((2, 2, 1, ROWS)),
+            vmem((2, 2, 1, ROWS)),
+            vmem((9, 1, N)),
+            vmem((9, 1, N)),
+            vmem((5, 1, ROWS)),
+            vmem((5, 1, ROWS)),
             pltpu.SemaphoreType.DMA((14,)),
             pltpu.SemaphoreType.DMA((3,)),
             pltpu.SemaphoreType.DMA((3,)),
-            pltpu.SemaphoreType.DMA((4, 4)),
-            pltpu.SemaphoreType.DMA((4, 4)),
+            pltpu.SemaphoreType.DMA((2, 4)),
+            pltpu.SemaphoreType.DMA((2, 4)),
+            pltpu.SemaphoreType.DMA((7,)),
+            pltpu.SemaphoreType.DMA((7,)),
         ],
         compiler_params=pltpu.CompilerParams(
-            collective_id=0, has_side_effects=True, vmem_limit_bytes=40 * 2**20
+            collective_id=0, has_side_effects=True, vmem_limit_bytes=60 * 2**20
         ),
     )(
-        rhs_matrix,
-        trans_x,
-        trans_y,
-        leak_matrix,
-        rhs_fracture,
-        trans_frac,
-        store_frac,
-        mortar_coef,
-        block_home.T,
-        block_len.reshape(1, N),
-        mortar_cell.T,
-        cross_cell.T,
-        cross_partner.T,
-        cross_trans.T,
+        *[
+            pltpu.with_memory_space_constraint(operand, pltpu.HBM)
+            for operand in (
+                rhs_matrix,
+                trans_x,
+                trans_y,
+                leak_matrix,
+                rhs_fracture,
+                trans_frac,
+                store_frac,
+                mortar_coef,
+                block_home.T,
+                block_len.reshape(1, N),
+                mortar_cell.T,
+                cross_cell.T,
+                cross_partner.T,
+                cross_trans.T,
+            )
+        ]
     )
+    return pl.pallas_call(
+        combine,
+        out_shape=(
+            jax.ShapeDtypeStruct(tile, F32),
+            jax.ShapeDtypeStruct(block, F32),
+            jax.ShapeDtypeStruct(block, F32),
+        ),
+        in_specs=[pl.BlockSpec(memory_space=pltpu.VMEM)] * 3,
+        out_specs=(pl.BlockSpec(memory_space=pl.ANY),) * 3,
+        scratch_shapes=[vmem(tile), vmem(block), vmem(block), pltpu.SemaphoreType.DMA((3,))],
+    )(*[pltpu.with_memory_space_constraint(result, pltpu.VMEM) for result in results])
 
 
 def solution(mesh):

time: 51.1 us -> 37.6 us (0.74)
  local copies, waits for them, and re-layouts: 9.58 us -> 0 us
  Pallas kernels: 40.4 us -> 36.8 us
    unnamed x31 -> x0, local copies, waits for them, and re-layouts: 9.58 us -> none
    pallas_call x1 -> x2, Pallas kernels: 40.4 us -> 36.8 us  [the longest x1 36.1 us: local(): pl.pallas_call(kernel, out_shape=(vmem((3,) + tile), vmem((5,) + block),...]
where the time goes in v2:
time: 37.6 us; the launch traced here: 37.5 us
  Pallas kernels  36.8 us (98%)
  between operations  0.64 us (2%)
    pallas_call x1, Pallas kernels, local(): pl.pallas_call(kernel, out_shape=(vmem((3,) + tile), vmem((5,) + block),...  36.1 us

profile of v2, /device:TPU:1, one launch (start us, length us, event | category | flops | bytes accessed | tf_op | source)
XLA Modules:
  0.0 37.5 jit_solution(7862858814688786062)
XLA Ops:
  0.6 36.1 %shard_map.157 = (f32[3,256,128]{2,1,0:T(8,128)S(1)}, f32[5,128,128]{2,1,0:T(8,128)S(1)}, f32[8,128]{1,0:T(8,128)S(1)}) custom-call(f32[256,128]{1,0:T(8,128)} %rhs_m_hbm.1, f32[256,128]{1,0:T(8,128)} %tx_hbm.1, f32[256,128]{1,0:T(8,128)} %ty_hbm.1, f32[256,128]{1,0:T(8,128)} %leak_hbm.1, f32[128,128]{1,0:T(8,128)} %rhs_f_hbm.1, f32[128,128]{1,0:T(8,128)} %tf_hbm.1, ...), custom_call_target="tpu_custom_call" | custom-call | tf_op jit(solution)/shard_map/pallas_call | solution.py:595
  36.7 0.7 %shard_map.158 = (f32[256,128]{1,0:T(8,128)}, f32[128,128]{1,0:T(8,128)}, f32[128,128]{1,0:T(8,128)}) custom-call(f32[3,256,128]{2,1,0:T(8,128)S(1)} %get-tuple-element.6.pm, f32[5,128,128]{2,1,0:T(8,128)S(1)} %get-tuple-element.7.fm, f32[8,128]{1,0:T(8,128)S(1)} %get-tuple-element.8.factors), custom_call_target="tpu_custom_call" | custom-call | tf_op jit(solution)/shard_map/pallas_call | solution.py:654

commit v3 on v2

--- a/solution.py
+++ b/solution.py
@@ -12,10 +12,9 @@
 N = 128
 ROWS = 256
 BAND = 64
-ROWS0 = 9
-ROWS1 = 6
-
-FIRST = 100
+ROWS0 = 5
+ROWS1 = 4
+ROWS3 = 6
 
 HOPS = (0, 1, 2, 1)
 OFFSETS = sorted(
@@ -40,6 +39,13 @@
 
 
 def pick(hot, fields):
+    if hot.shape[1] == N:
+        columns = jnp.concatenate(fields, axis=1)
+        stacked = jnp.concatenate(split(columns), axis=0)
+        out = jnp.dot(
+            jnp.concatenate([hot] * 3, axis=1), stacked, preferred_element_type=F32
+        )
+        return [out[:, N * i : N * (i + 1)] for i in range(len(fields))]
     parts = [part for field in fields for part in split(field)]
     out = jnp.dot(hot, jnp.concatenate(parts, axis=1), preferred_element_type=F32)
     n = fields[0].shape[1]
@@ -98,6 +104,8 @@
     recv1,
     send2,
     recv2,
+    send3,
+    recv3,
     hsend_r,
     hrecv_r,
     hsend_c,
@@ -243,12 +251,17 @@
     mcell_row = mcell[...].astype(F32)
     cells = [jnp.sum(s * mcell_row, axis=1, keepdims=True) for s in slots]
     slot_hot = jnp.concatenate(slots, axis=0).astype(BF16)
-    packed = pick(slot_hot, [inv_l, ratio_l, q0, q1])
-    for i, value in enumerate(packed):
+    q2_part = -inv_f * off_f(q1)
+    packed = pick(slot_hot, [inv_l, q0, ratio_l, q1, q2_part])
+    for i, value in enumerate(packed[:2]):
         send0[:, 2 * i, :] = value[:N]
         send0[:, 2 * i + 1, :] = value[N:]
-    send0[:, 8, :] = jnp.where(lane < BAND, cells[0], cells[1])
+    send0[:, 4, :] = jnp.where(lane < BAND, cells[0], cells[1])
+    for i, value in enumerate(packed[2:]):
+        send3[:, 2 * i, :] = value[:N]
+        send3[:, 2 * i + 1, :] = value[N:]
     recv0[pl.ds(me, 1)] = send0[pl.ds(me, 1)]
+    recv3[pl.ds(me, 1)] = send3[pl.ds(me, 1)]
 
     fm[0] = q0
     fm[1] = q1
@@ -261,11 +274,13 @@
         ((sub8 == 0) & (lane8 == 0)) | ((sub8 == 1) & (lane8 == N - 1)), 1.0, 0.0
     ).astype(BF16)
 
-    def end_cols(fields):
-        parts = jnp.concatenate([part for field in fields for part in split(field)], axis=0)
-        out = lax.dot_general(ends, parts, (((1,), (1,)), ((), ())), preferred_element_type=F32)
-        pieces = [out[:, ROWS * k : ROWS * (k + 1)] for k in range(3 * len(fields))]
-        return [pieces[3 * k] + pieces[3 * k + 1] + pieces[3 * k + 2] for k in range(len(fields))]
+    def end_cols(field):
+        return lax.dot_general(
+            jnp.concatenate([ends] * 3, axis=1),
+            jnp.concatenate(split(field), axis=1),
+            (((1,), (1,)), ((), ())),
+            preferred_element_type=F32,
+        )
 
     def halo_copy(phase, way):
         device = (below, above, right, left)[way]
@@ -279,10 +294,9 @@
             device_id_type=LOGICAL,
         )
 
-    def halo_send(phase, field):
-        hsend_r[phase, 0] = field[ROWS - 1 : ROWS]
-        hsend_r[phase, 1] = field[0:1]
-        cols = end_cols([field])[0]
+    def halo_send(phase, first, last, cols):
+        hsend_r[phase, 0] = last
+        hsend_r[phase, 1] = first
         hsend_c[phase, 0] = cols[1:2]
         hsend_c[phase, 1] = cols[0:1]
         for way in range(4):
@@ -320,7 +334,7 @@
     esend_r[6] = ty[ROWS - 1 : ROWS]
     esend_r[7] = ty[0:1]
     esend_r[8] = tx[ROWS - 1 : ROWS]
-    ty_cols, rhs_cols, partial_cols = end_cols([ty[...], rhs_m[...], partial])
+    ty_cols, rhs_cols, partial_cols = end_cols(ty[...]), end_cols(rhs_m[...]), end_cols(partial)
     esend_c[0] = ty_cols[1:2]
     esend_c[1] = rhs_cols[1:2]
     esend_c[2] = partial_cols[1:2]
@@ -350,19 +364,19 @@
     for i in range(7):
         edge_copy(i).start()
 
-    def send_to_home(o):
+    def send_to(o, send, recv, i):
         t = target(o)
         pltpu.make_async_remote_copy(
-            send0.at[t],
-            recv0.at[me],
-            ssem.at[0],
-            rsem.at[0],
+            send.at[t],
+            recv.at[me],
+            ssem.at[i],
+            rsem.at[i],
             device_id=t,
             device_id_type=LOGICAL,
         ).start()
 
-    for o in OFFSETS[:FIRST]:
-        send_to_home(o)
+    for o in OFFSETS:
+        send_to(o, send0, recv0, 0)
 
     for i in range(7):
         edge_copy(i).wait_recv()
@@ -399,15 +413,12 @@
     co[4] = diag_m
     co[5] = inv_m
     p1 = -off_m(pm[0], p0_above, p0_below, p0_left, p0_right)
-    halo_send(0, p1)
+    halo_send(0, p1[0:1], p1[ROWS - 1 : ROWS], end_cols(p1))
     pm[1] = p1
-
-    for o in OFFSETS[FIRST:]:
-        send_to_home(o)
+    for o in OFFSETS:
+        send_to(o, send3, recv3, 3)
 
     slot_hot_t = jnp.concatenate([s.T for s in slots], axis=1).astype(BF16)
-    q2_part = -inv_f * off_f(fm[1])
-    pm[2] = -off_m(pm[1], *halo(0))
     dm = co[4]
     moments = [
         fold(dm * pm[0] * pm[0]) + fold(safe * fm[0] * fm[0]),
@@ -427,129 +438,121 @@
 
     all_arrived(send0, recv0, 0).wait_recv()
     lane_band = jnp.where(lane < BAND, lane, lane - BAND).astype(F32)
-    hit = jnp.where(recv0[:, 8, :] == lane_band, 1.0, 0.0)
+    hit = jnp.where(recv0[:, 4, :] == lane_band, 1.0, 0.0)
     hit_slots = jnp.concatenate(
         [jnp.where(lane < BAND, hit, 0.0), jnp.where(lane < BAND, 0.0, hit)], axis=0
     ).astype(BF16)
-    hit_t = hit.T
-    hit_rows = jnp.concatenate([hit_t[:BAND], hit_t[BAND:]], axis=1).astype(BF16)
 
     def sample(fields):
         return pick(hit_slots, [jnp.concatenate([f, f], axis=0) for f in fields])
 
     p0_at, p1_at = sample([pm[0, 0:BAND], pm[1, 0:BAND]])
-
-    def both(r):
-        return jnp.concatenate([recv0[:, r, :], recv0[:, r + 1, :]], axis=0)
-
-    inv_at, ratio_at = both(0), both(2)
-    l1 = inv_at * (p0_at - both(4))
-    l2 = inv_at * (p1_at - both(6)) - (ratio_at + 1.0) * l1
-    pm[2, 0:BAND] += co[5, 0:BAND] * pick(hit_rows, [l1])[0]
-    p2 = pm[2]
-    halo_send(1, p2)
-    p2_at = sample([p2[0:BAND]])[0]
-    for i, value in enumerate((l1, l2, p2_at)):
+    for i, value in enumerate((p0_at, p1_at)):
         send1[:, 2 * i, :] = value[:N]
         send1[:, 2 * i + 1, :] = value[N:]
     recv1[pl.ds(me, 1)] = send1[pl.ds(me, 1)]
     for o in OFFSETS:
-        t = target(o)
-        pltpu.make_async_remote_copy(
-            send1.at[t],
-            recv1.at[me],
-            ssem.at[1],
-            rsem.at[1],
-            device_id=t,
-            device_id_type=LOGICAL,
-        ).start()
+        send_to(o, send1, recv1, 1)
+
+    hit_t = hit.T
+    hit_rows = jnp.concatenate([hit_t[:BAND], hit_t[BAND:]], axis=1).astype(BF16)
+
+    def both(ref, r):
+        return jnp.concatenate([ref[:, r, :], ref[:, r + 1, :]], axis=0)
+
+    inv_at = both(recv0, 0)
+    l1 = inv_at * (p0_at - both(recv0, 2))
+    p2_part = -off_m(pm[1], *halo(0))
+    part_cols = end_cols(p2_part)
+    pushed = co[5, 0:BAND] * pick(hit_rows, [l1])[0]
+    pm[2] = p2_part
+    pm[2, 0:BAND] += pushed
+    pushed_cols = jnp.concatenate(
+        [end_cols(pushed), jnp.zeros((8, ROWS - BAND), F32)], axis=1
+    )
+    halo_send(
+        1,
+        p2_part[0:1] + pushed[0:1],
+        p2_part[ROWS - 1 : ROWS],
+        part_cols + pushed_cols,
+    )
+    p2 = pm[2]
+    p2_at = sample([p2[0:BAND]])[0]
+    all_arrived(send3, recv3, 3).wait_recv()
+    ratio_at = both(recv3, 0)
+    l2 = inv_at * (p1_at - both(recv3, 2)) - (1.0 + ratio_at) * l1
+    l3 = inv_at * (p2_at - both(recv3, 4)) + (1.0 - ratio_at) * l1 - (1.0 + ratio_at) * l2
+    metric_at = jnp.where(inv_at > 0.0, 1.0 / inv_at, 0.0)
+    m1, m2 = metric_at * l1, metric_at * l2
+    moments[2] += fold(m1 * l1)
+    moments.append(fold(m1 * l2))
+    moments.append(fold(m2 * l2))
+    moments.append(fold(m2 * l3))
+    moments.append(fold(metric_at * l3 * l3))
+    d2 = co[4] * pm[2]
+    moments[3] += fold(d2 * pm[1])
+    moments[4] += fold(d2 * pm[2])
     p3_ref[...] = -off_m(pm[2], *halo(1))
     p3_ref[0:BAND] += co[5, 0:BAND] * pick(hit_rows, [l2])[0]
-    d2 = co[4] * pm[2]
-    moments.append(fold(d2 * pm[1]))
-    moments.append(fold(d2 * pm[2]))
     p3 = p3_ref[...]
-    moments.append(fold(d2 * p3))
-    moments.append(fold(co[4] * p3 * p3))
+    moments[5] += fold(d2 * p3)
+    moments[6] += fold(co[4] * p3 * p3)
 
     all_arrived(send1, recv1, 1).wait_recv()
 
     def returned(r):
         return jnp.concatenate([recv1[:, r, :], recv1[:, r + 1, :]], axis=0)
 
-    l1, l2, p2_at = pick(slot_hot_t, [returned(0), returned(2), returned(4)])
+    p0_at, p1_at = pick(slot_hot_t, [returned(0), returned(2)])
+    l1 = inv_l * (p0_at - fm[0])
+    l2 = inv_l * (p1_at - fm[1]) - (1.0 + ratio_l) * l1
     q2 = q2_part - inv_f * l1
     q3 = -inv_f * (off_f(q2) + l2)
-    l3 = inv_l * (p2_at - q2) - (ratio_l + 1.0) * l2
     fm[2] = q2
     fm[3] = l1
     fm[4] = l2
-    m1, m2 = metric_l * l1, metric_l * l2
     s2 = safe * q2
-    moments[2] += fold(m1 * l1)
-    moments[3] += fold(s2 * fm[1] + m1 * l2)
-    moments[4] += fold(s2 * q2 + m2 * l2)
-    moments[5] += fold(s2 * q3 + m2 * l3)
-    moments[6] += fold(safe * q3 * q3 + metric_l * l3 * l3)
+    moments[3] += fold(s2 * fm[1])
+    moments[4] += fold(s2 * q2)
+    moments[5] += fold(s2 * q3)
+    moments[6] += fold(safe * q3 * q3)
     rows = [jnp.sum(m, axis=0, keepdims=True) for m in moments]
     sums = jnp.sum(jnp.concatenate(rows + [jnp.zeros((1, N), F32)], axis=0), axis=1, keepdims=True)
     mine = jnp.sum(jnp.where(lane8 == sub8, sums, 0.0), axis=0, keepdims=True)
-    send2[...] = mine
-    recv2[pl.ds(me, 1)] = mine[None]
+    send2[0:1] = mine
+    recv2[pl.ds(me, 1), 0:1] = mine[None]
     for o in OFFSETS:
         pltpu.make_async_remote_copy(
-            send2,
-            recv2.at[me],
+            send2.at[0:1],
+            recv2.at[me, 0:1],
             ssem.at[2],
             rsem.at[2],
             device_id=target(o),
             device_id_type=LOGICAL,
         ).start()
-    all_arrived(recv2, recv2, 2).wait_recv()
-    total = jnp.sum(recv2[...], axis=0)
+    all_arrived(recv2.at[:, 0:1], recv2.at[:, 0:1], 2).wait_recv()
+    total = jnp.sum(fold(recv2[:, 0, :]), axis=0, keepdims=True)
     mu = [jnp.broadcast_to(total[:, i : i + 1], (1, N)) for i in range(7)]
 
-    n0 = mu[0]
-    a0 = mu[1] / n0
-    n1 = mu[2] - a0 * mu[1]
-    a1 = (mu[3] - a0 * (mu[2] + n1)) / n1
-    b1 = n1 / n0
-    c1 = -(a0 + a1)
-    c0 = a0 * a1 - b1
-    n2 = mu[4] + c1 * mu[3] + c0 * mu[2]
-    a2 = (mu[5] + c1 * mu[4] + c0 * mu[3]) / n2 + c1
-    b2 = n2 / n1
-    square = mu[6] + 2.0 * c1 * mu[5] + (c1 * c1 + 2.0 * c0) * mu[4] + 2.0 * c0 * c1 * mu[3] + c0 * c0 * mu[2]
-    n3 = square - (a2 * a2 + b2) * n2
-    gammas = [jnp.sqrt(n0), jnp.sqrt(b1), jnp.sqrt(b2), jnp.sqrt(n3 / n2)]
-    curvatures = [a0 + 1.0, a1 + 1.0, a2 + 1.0]
-    i0, i1, i2 = lax.rsqrt(n0), lax.rsqrt(n1), lax.rsqrt(n2)
-    zero = jnp.zeros_like(n0)
-    one = jnp.ones_like(n0)
-    basis = [(i0, zero, zero), (-a0 * i1, i1, zero), (c0 * i2, c1 * i2, i2)]
-    cos_old, cos_now, sin_old, sin_now = one, one, zero, zero
-    rhs_scale = gammas[0]
-    search_old = search_now = iterate = (zero, zero, zero)
-    for k in range(3):
-        gamma, gamma_new = gammas[k], gammas[k + 1]
-        alpha_zero = cos_now * curvatures[k] - cos_old * sin_now * gamma
-        alpha_one = jnp.sqrt(alpha_zero * alpha_zero + gamma_new * gamma_new)
-        alpha_two = sin_now * curvatures[k] + cos_old * cos_now * gamma
-        alpha_three = sin_old * gamma
-        cos_new, sin_new = alpha_zero / alpha_one, gamma_new / alpha_one
-        search_new = tuple(
-            (z - alpha_three * old - alpha_two * now) / alpha_one
-            for z, old, now in zip(basis[k], search_old, search_now)
-        )
-        iterate = tuple(x + cos_new * rhs_scale * w for x, w in zip(iterate, search_new))
-        rhs_scale = -sin_new * rhs_scale
-        cos_old, cos_now, sin_old, sin_now = cos_now, cos_new, sin_now, sin_new
-        search_old, search_now = search_now, search_new
-    factors[...] = jnp.concatenate(list(iterate) + [zero] * 5, axis=0)
+    gram = [mu[k] + 2.0 * mu[k + 1] + mu[k + 2] for k in range(5)]
+    right_side = [mu[k] + mu[k + 1] for k in range(3)]
+    i0 = 1.0 / gram[0]
+    l10, l20 = gram[1] * i0, gram[2] * i0
+    i1 = 1.0 / (gram[2] - l10 * gram[1])
+    off = gram[3] - l20 * gram[1]
+    l21 = off * i1
+    i2 = 1.0 / (gram[4] - l20 * gram[2] - l21 * off)
+    y1 = right_side[1] - l10 * right_side[0]
+    y2 = right_side[2] - l20 * right_side[0] - l21 * y1
+    x2 = y2 * i2
+    x1 = y1 * i1 - l21 * x2
+    x0 = right_side[0] * i0 - l10 * x1 - l20 * x2
+    factors[...] = jnp.concatenate([x0, x1, x2, jnp.zeros((5, N), F32)], axis=0)
 
     all_arrived(send0, recv0, 0).wait_send()
     all_arrived(send1, recv1, 1).wait_send()
-    all_arrived(recv2, recv2, 2).wait_send()
+    all_arrived(recv2.at[:, 0:1], recv2.at[:, 0:1], 2).wait_send()
+    all_arrived(send3, recv3, 3).wait_send()
     for i in range(7):
         edge_copy(i).wait_send()
     for phase in range(2):
@@ -609,8 +612,10 @@
             vmem((N, ROWS0, N)),
             vmem((N, ROWS1, N)),
             vmem((N, ROWS1, N)),
-            vmem((1, N)),
-            vmem((N, 1, N)),
+            vmem((8, N)),
+            vmem((N, 8, N)),
+            vmem((N, ROWS3, N)),
+            vmem((N, ROWS3, N)),
             vmem((2, 2, 1, N)),
             vmem((2, 2, 1, N)),
             vmem((2, 2, 1, ROWS)),
@@ -620,8 +625,8 @@
             vmem((5, 1, ROWS)),
             vmem((5, 1, ROWS)),
             pltpu.SemaphoreType.DMA((14,)),
-            pltpu.SemaphoreType.DMA((3,)),
-            pltpu.SemaphoreType.DMA((3,)),
+            pltpu.SemaphoreType.DMA((4,)),
+            pltpu.SemaphoreType.DMA((4,)),
             pltpu.SemaphoreType.DMA((2, 4)),
             pltpu.SemaphoreType.DMA((2, 4)),
             pltpu.SemaphoreType.DMA((7,)),

time: 37.6 us -> 34.5 us (0.918)
  Pallas kernels: 36.8 us -> 33.8 us
    pallas_call x1, Pallas kernels: 36.1 us -> 33 us  [local(): pl.pallas_call(kernel, out_shape=(vmem((3,) + tile), vmem((5,) + block),...]
where the time goes in v3:
time: 34.5 us; the launch traced here: 34.4 us
  Pallas kernels  33.8 us (98%)
  between operations  0.64 us (2%)
    pallas_call x1, Pallas kernels, local(): pl.pallas_call(kernel, out_shape=(vmem((3,) + tile), vmem((5,) + block),...  33 us
    pallas_call x1, Pallas kernels, local(): pl.pallas_call(combine, out_shape=(jax.ShapeDtypeStruct(tile, F32), jax.S...  0.75 us

profile of v3, /device:TPU:1, one launch (start us, length us, event | category | flops | bytes accessed | tf_op | source)
XLA Modules:
  0.0 34.4 jit_solution(6448958010397924785)
XLA Ops:
  0.6 33.0 %shard_map.157 = (f32[3,256,128]{2,1,0:T(8,128)S(1)}, f32[5,128,128]{2,1,0:T(8,128)S(1)}, f32[8,128]{1,0:T(8,128)S(1)}) custom-call(f32[256,128]{1,0:T(8,128)} %rhs_m_hbm.1, f32[256,128]{1,0:T(8,128)} %tx_hbm.1, f32[256,128]{1,0:T(8,128)} %ty_hbm.1, f32[256,128]{1,0:T(8,128)} %leak_hbm.1, f32[128,128]{1,0:T(8,128)} %rhs_f_hbm.1, f32[128,128]{1,0:T(8,128)} %tf_hbm.1, ...), custom_call_target="tpu_custom_call" | custom-call | tf_op jit(solution)/shard_map/pallas_call | solution.py:598
  33.6 0.7 %shard_map.158 = (f32[256,128]{1,0:T(8,128)}, f32[128,128]{1,0:T(8,128)}, f32[128,128]{1,0:T(8,128)}) custom-call(f32[3,256,128]{2,1,0:T(8,128)S(1)} %get-tuple-element.6.pm, f32[5,128,128]{2,1,0:T(8,128)S(1)} %get-tuple-element.7.fm, f32[8,128]{1,0:T(8,128)S(1)} %get-tuple-element.8.factors), custom_call_target="tpu_custom_call" | custom-call | tf_op jit(solution)/shard_map/pallas_call | solution.py:659

commit v4 on v3

--- a/solution.py
+++ b/solution.py
@@ -14,7 +14,8 @@
 BAND = 64
 ROWS0 = 5
 ROWS1 = 4
-ROWS3 = 6
+ROWS3 = 4
+ROWS4 = 2
 
 HOPS = (0, 1, 2, 1)
 OFFSETS = sorted(
@@ -106,6 +107,8 @@
     recv2,
     send3,
     recv3,
+    send4,
+    recv4,
     hsend_r,
     hrecv_r,
     hsend_c,
@@ -257,11 +260,14 @@
         send0[:, 2 * i, :] = value[:N]
         send0[:, 2 * i + 1, :] = value[N:]
     send0[:, 4, :] = jnp.where(lane < BAND, cells[0], cells[1])
-    for i, value in enumerate(packed[2:]):
+    send4[:, 0, :] = packed[4][:N]
+    send4[:, 1, :] = packed[4][N:]
+    for i, value in enumerate(packed[2:4]):
         send3[:, 2 * i, :] = value[:N]
         send3[:, 2 * i + 1, :] = value[N:]
     recv0[pl.ds(me, 1)] = send0[pl.ds(me, 1)]
     recv3[pl.ds(me, 1)] = send3[pl.ds(me, 1)]
+    recv4[pl.ds(me, 1)] = send4[pl.ds(me, 1)]
 
     fm[0] = q0
     fm[1] = q1
@@ -476,27 +482,27 @@
         p2_part[ROWS - 1 : ROWS],
         part_cols + pushed_cols,
     )
+    for o in OFFSETS:
+        send_to(o, send4, recv4, 4)
     p2 = pm[2]
     p2_at = sample([p2[0:BAND]])[0]
     all_arrived(send3, recv3, 3).wait_recv()
     ratio_at = both(recv3, 0)
     l2 = inv_at * (p1_at - both(recv3, 2)) - (1.0 + ratio_at) * l1
-    l3 = inv_at * (p2_at - both(recv3, 4)) + (1.0 - ratio_at) * l1 - (1.0 + ratio_at) * l2
     metric_at = jnp.where(inv_at > 0.0, 1.0 / inv_at, 0.0)
     m1, m2 = metric_at * l1, metric_at * l2
     moments[2] += fold(m1 * l1)
     moments.append(fold(m1 * l2))
     moments.append(fold(m2 * l2))
-    moments.append(fold(m2 * l3))
-    moments.append(fold(metric_at * l3 * l3))
     d2 = co[4] * pm[2]
     moments[3] += fold(d2 * pm[1])
     moments[4] += fold(d2 * pm[2])
     p3_ref[...] = -off_m(pm[2], *halo(1))
     p3_ref[0:BAND] += co[5, 0:BAND] * pick(hit_rows, [l2])[0]
     p3 = p3_ref[...]
-    moments[5] += fold(d2 * p3)
-    moments[6] += fold(co[4] * p3 * p3)
+    moments.append(fold(d2 * p3))
+    moments.append(fold(co[4] * p3 * p3))
+    l3_part = inv_at * p2_at + (1.0 - ratio_at) * l1 - (1.0 + ratio_at) * l2
 
     all_arrived(send1, recv1, 1).wait_recv()
 
@@ -516,6 +522,10 @@
     moments[4] += fold(s2 * q2)
     moments[5] += fold(s2 * q3)
     moments[6] += fold(safe * q3 * q3)
+    all_arrived(send4, recv4, 4).wait_recv()
+    l3 = l3_part - inv_at * both(recv4, 0)
+    moments[5] += fold(m2 * l3)
+    moments[6] += fold(metric_at * l3 * l3)
     rows = [jnp.sum(m, axis=0, keepdims=True) for m in moments]
     sums = jnp.sum(jnp.concatenate(rows + [jnp.zeros((1, N), F32)], axis=0), axis=1, keepdims=True)
     mine = jnp.sum(jnp.where(lane8 == sub8, sums, 0.0), axis=0, keepdims=True)
@@ -553,6 +563,7 @@
     all_arrived(send1, recv1, 1).wait_send()
     all_arrived(recv2.at[:, 0:1], recv2.at[:, 0:1], 2).wait_send()
     all_arrived(send3, recv3, 3).wait_send()
+    all_arrived(send4, recv4, 4).wait_send()
     for i in range(7):
         edge_copy(i).wait_send()
     for phase in range(2):
@@ -616,6 +627,8 @@
             vmem((N, 8, N)),
             vmem((N, ROWS3, N)),
             vmem((N, ROWS3, N)),
+            vmem((N, ROWS4, N)),
+            vmem((N, ROWS4, N)),
             vmem((2, 2, 1, N)),
             vmem((2, 2, 1, N)),
             vmem((2, 2, 1, ROWS)),
@@ -625,8 +638,8 @@
             vmem((5, 1, ROWS)),
             vmem((5, 1, ROWS)),
             pltpu.SemaphoreType.DMA((14,)),
-            pltpu.SemaphoreType.DMA((4,)),
-            pltpu.SemaphoreType.DMA((4,)),
+            pltpu.SemaphoreType.DMA((5,)),
+            pltpu.SemaphoreType.DMA((5,)),
             pltpu.SemaphoreType.DMA((2, 4)),
             pltpu.SemaphoreType.DMA((2, 4)),
             pltpu.SemaphoreType.DMA((7,)),

time: 34.5 us -> 34 us (0.986)
  Pallas kernels: 33.8 us -> 33.3 us
    pallas_call x1, Pallas kernels: 33 us -> 32.5 us  [local(): pl.pallas_call(kernel, out_shape=(vmem((3,) + tile), vmem((5,) + block),...]
where the time goes in v4:
time: 34 us; the launch traced here: 33.9 us
  Pallas kernels  33.3 us (98%)
  between operations  0.64 us (2%)
    pallas_call x1, Pallas kernels, local(): pl.pallas_call(kernel, out_shape=(vmem((3,) + tile), vmem((5,) + block),...  32.5 us
    pallas_call x1, Pallas kernels, local(): pl.pallas_call(combine, out_shape=(jax.ShapeDtypeStruct(tile, F32), jax.S...  0.75 us

profile of v4, /device:TPU:1, one launch (start us, length us, event | category | flops | bytes accessed | tf_op | source)
XLA Modules:
  0.0 33.9 jit_solution(4891198256104398431)
XLA Ops:
  0.6 32.5 %shard_map.157 = (f32[3,256,128]{2,1,0:T(8,128)S(1)}, f32[5,128,128]{2,1,0:T(8,128)S(1)}, f32[8,128]{1,0:T(8,128)S(1)}) custom-call(f32[256,128]{1,0:T(8,128)} %rhs_m_hbm.1, f32[256,128]{1,0:T(8,128)} %tx_hbm.1, f32[256,128]{1,0:T(8,128)} %ty_hbm.1, f32[256,128]{1,0:T(8,128)} %leak_hbm.1, f32[128,128]{1,0:T(8,128)} %rhs_f_hbm.1, f32[128,128]{1,0:T(8,128)} %tf_hbm.1, ...), custom_call_target="tpu_custom_call" | custom-call | tf_op jit(solution)/shard_map/pallas_call | solution.py:609
  33.2 0.7 %shard_map.158 = (f32[256,128]{1,0:T(8,128)}, f32[128,128]{1,0:T(8,128)}, f32[128,128]{1,0:T(8,128)}) custom-call(f32[3,256,128]{2,1,0:T(8,128)S(1)} %get-tuple-element.6.pm, f32[5,128,128]{2,1,0:T(8,128)S(1)} %get-tuple-element.7.fm, f32[8,128]{1,0:T(8,128)S(1)} %get-tuple-element.8.factors), custom_call_target="tpu_custom_call" | custom-call | tf_op jit(solution)/shard_map/pallas_call | solution.py:672

commit v5 on v4

--- a/solution.py
+++ b/solution.py
@@ -33,10 +33,7 @@
 
 def split(value):
     high = value.astype(BF16)
-    rest = value - high.astype(F32)
-    middle = rest.astype(BF16)
-    low = (rest - middle.astype(F32)).astype(BF16)
-    return [high, middle, low]
+    return [high, (value - high.astype(F32)).astype(BF16)]
 
 
 def pick(hot, fields):
@@ -44,16 +41,14 @@
         columns = jnp.concatenate(fields, axis=1)
         stacked = jnp.concatenate(split(columns), axis=0)
         out = jnp.dot(
-            jnp.concatenate([hot] * 3, axis=1), stacked, preferred_element_type=F32
+            jnp.concatenate([hot] * 2, axis=1), stacked, preferred_element_type=F32
         )
         return [out[:, N * i : N * (i + 1)] for i in range(len(fields))]
     parts = [part for field in fields for part in split(field)]
     out = jnp.dot(hot, jnp.concatenate(parts, axis=1), preferred_element_type=F32)
     n = fields[0].shape[1]
     return [
-        out[:, 3 * n * i : 3 * n * i + n]
-        + out[:, 3 * n * i + n : 3 * n * i + 2 * n]
-        + out[:, 3 * n * i + 2 * n : 3 * n * i + 3 * n]
+        out[:, 2 * n * i : 2 * n * i + n] + out[:, 2 * n * i + n : 2 * n * i + 2 * n]
         for i in range(len(fields))
     ]
 
@@ -282,7 +277,7 @@
 
     def end_cols(field):
         return lax.dot_general(
-            jnp.concatenate([ends] * 3, axis=1),
+            jnp.concatenate([ends] * 2, axis=1),
             jnp.concatenate(split(field), axis=1),
             (((1,), (1,)), ((), ())),
             preferred_element_type=F32,
@@ -367,7 +362,7 @@
         )
 
     pl.semaphore_wait(barrier, N - 1)
-    for i in range(7):
+    for i in (2, 3, 4, 0, 1, 5, 6):
         edge_copy(i).start()
 
     def send_to(o, send, recv, i):

time: 34 us -> 34.2 us (level)
  no operation moved by 1% of the time
where the time goes in v5:
time: 34.2 us; the launch traced here: 34.1 us
  Pallas kernels  33.4 us (98%)
  between operations  0.64 us (2%)
    pallas_call x1, Pallas kernels, local(): pl.pallas_call(kernel, out_shape=(vmem((3,) + tile), vmem((5,) + block),...  32.7 us
    pallas_call x1, Pallas kernels, local(): pl.pallas_call(combine, out_shape=(jax.ShapeDtypeStruct(tile, F32), jax.S...  0.75 us

profile of v5, /device:TPU:1, one launch (start us, length us, event | category | flops | bytes accessed | tf_op | source)
XLA Modules:
  0.0 34.1 jit_solution(3061617214318814539)
XLA Ops:
  0.6 32.7 %shard_map.157 = (f32[3,256,128]{2,1,0:T(8,128)S(1)}, f32[5,128,128]{2,1,0:T(8,128)S(1)}, f32[8,128]{1,0:T(8,128)S(1)}) custom-call(f32[256,128]{1,0:T(8,128)} %rhs_m_hbm.1, f32[256,128]{1,0:T(8,128)} %tx_hbm.1, f32[256,128]{1,0:T(8,128)} %ty_hbm.1, f32[256,128]{1,0:T(8,128)} %leak_hbm.1, f32[128,128]{1,0:T(8,128)} %rhs_f_hbm.1, f32[128,128]{1,0:T(8,128)} %tf_hbm.1, ...), custom_call_target="tpu_custom_call" | custom-call | tf_op jit(solution)/shard_map/pallas_call | solution.py:604
  33.3 0.7 %shard_map.158 = (f32[256,128]{1,0:T(8,128)}, f32[128,128]{1,0:T(8,128)}, f32[128,128]{1,0:T(8,128)}) custom-call(f32[3,256,128]{2,1,0:T(8,128)S(1)} %get-tuple-element.6.pm, f32[5,128,128]{2,1,0:T(8,128)S(1)} %get-tuple-element.7.fm, f32[8,128]{1,0:T(8,128)S(1)} %get-tuple-element.8.factors), custom_call_target="tpu_custom_call" | custom-call | tf_op jit(solution)/shard_map/pallas_call | solution.py:667
